TPU v7x, 256 devices: a whole 4x4x8 slice. The times are simulated.
256 devices in a mesh: occ: 64 (over y_lo, z, x), vir: 4 (over y_hi, core).
Axes of the slice: x: 4, y: 4 (y_hi: 2, y_lo: 2; y = y_hi * 2 + y_lo), z: 8, core: 2. Of those that a mesh axis runs over, the one named last changes fastest.
Arguments:
- amplitudes: float32 [32768, 2048], P('occ', 'vir'), may hold values from -6 to 6
- integrals: float32 [2048, 8192], P('vir', 'occ'), may hold values from -0.375 to 0.375
- ij_irrep: int32 [32768], P('occ'), may hold values from 0 to 7
- cd_irrep: int32 [2048], P('vir'), may hold values from 0 to 7
- ab_irrep: int32 [8192], P('occ'), may hold values from 0 to 7
Outputs:
- ladder: float32 [32768, 8192], P('occ', 'vir')
All inputs are finite; a program needn't handle non-finite values.
Results may differ from a plain program's by a relative error of at most 0.0003.
Values sent between devices are 32-bit elements; how exact they have to be, the bound alone decides.
A program may use at most 128 MiB of HBM per device.

v0:
```python
import jax
import jax.numpy as jnp
from jax import lax
from jax.sharding import PartitionSpec as P


def per_device(amplitudes, integrals, ij_irrep, cd_irrep, ab_irrep):
    t_sym = jnp.where(ij_irrep[:, None] == cd_irrep[None, :], amplitudes, jnp.float32(0.0))
    v_sym = jnp.where(cd_irrep[:, None] == ab_irrep[None, :], integrals, jnp.float32(0.0))
    partial_sum = jnp.dot(
        t_sym,
        lax.all_gather(v_sym, "occ", axis=1, tiled=True),
        preferred_element_type=jnp.float32,
        precision=lax.Precision.HIGHEST,
    )
    ladder = lax.psum_scatter(partial_sum, "vir", scatter_dimension=1, tiled=True)
    return ladder


def solution(mesh):
    in_specs = (P("occ", "vir"), P("vir", "occ"), P("occ"), P("vir"), P("occ"))
    out_specs = P("occ", "vir")
    return jax.shard_map(
        per_device, mesh=mesh, in_specs=in_specs, out_specs=out_specs, check_vma=False
    )
```

profile of v0, /device:TPU:1, one launch (start us, length us, event | category | flops | bytes accessed | tf_op | source)
XLA Modules:
  0.0 528.6 jit_solution(9785990908625707248)
XLA Ops:
  6.5 0.0 all-gather.2.cloned.1.call-start
  6.5 1.8 compare_select_fusion
  8.3 0.0 all-gather.2.cloned.1.call-update
  8.4 0.0 reduce-scatter.2.cloned.1.call-start
  8.4 299.5 %all-gather.2.cloned.1.call-done = f32[512,8192]{1,0:T(8,128)} async-done(((f32[512,128]{1,0:T(8,128)}), f32[512,8192]{1,0:T(8,128)}) %all-gather.2.cloned.1.call-update) | async-done | bytes 16777232 | tf_op jit(solution)/shard_map/all_gather | solution.py:12
  307.9 31.9 %fusion = f32[512,8192]{1,0:T(8,128)} fusion(f32[512,8192]{1,0:T(8,128)} %all-gather.2.cloned.1.call-done, f32[512,512]{1,0:T(8,128)} %param.5, s32[512]{0:T(512)} %param.8, s32[512]{0:T(512)} %param.7), kind=kOutput, calls=%fused_computation | convolution fusion | flops 25770328064 | bytes 34607104 | tf_op jit(solution)/shard_map/dot_general | solution.py:10
  339.8 0.0 reduce-scatter.2.cloned.1.call-update
  339.9 181.9 %reduce-scatter.2.cloned.1.call-done = f32[512,2048]{1,0:T(8,128)} async-done(((f32[512,8192]{1,0:T(8,128)}), f32[512,2048]{1,0:T(8,128)}) %reduce-scatter.2.cloned.1.call-update) | async-done | bytes 4194320 | tf_op jit(solution)/shard_map/reduce_scatter | solution.py:16
Async XLA Ops:
  6.5 301.4 %all-gather.2.cloned.1.call-start = ((), (), s32[]{:S(2)}) async-start(), calls=%async_computation.1 | async-start | bytes 17039360 | tf_op jit(solution)/shard_map/all_gather | solution.py:12
  8.4 513.4 %reduce-scatter.2.cloned.1.call-start = ((), (), s32[]{:S(2)}) async-start(), calls=%async_computation.2 | async-start | bytes 20971520 | tf_op jit(solution)/shard_map/reduce_scatter | solution.py:16
Sparse Core Ops, SparseCore 0:
  9.1 298.7 all-gather.1
  340.0 181.6 reduce-scatter.1
where the time goes:
time: 529 us
  waiting for transfers between devices  481 us (91%)
  matrix products  31.9 us (6%)
  between operations  13.4 us (3%)
    all_gather x1, waiting for transfers between devices, per_device(): lax.all_gather(v_sym, 'occ', axis=1, tiled=True)  299 us
    reduce_scatter x1, waiting for transfers between devices, per_device(): lax.psum_scatter(partial_sum, 'vir', scatter_dimension=1, tiled=True)  182 us
    dot_general x1, matrix products, per_device(): jnp.dot(t_sym, lax.all_gather(v_sym, 'occ', axis=1, tiled=True), preferre...  31.9 us
  transfers between devices with their start and end apart: 2, of which 2 were waited for; matrix products, arithmetic and copies ran while one was open for 0% of the time, Pallas kernels for 0%

commit v1 on v0

v1 whole, which is shorter than its diff:
```python
import functools

import jax
import jax.numpy as jnp
from jax import lax
from jax.experimental import pallas as pl
from jax.experimental.pallas import tpu as pltpu
from jax.sharding import PartitionSpec as P

MESH = pl.DeviceIdType.MESH
G = 8
CAP = 95
ROWS = CAP + 1
NX, NZ = 4, 8
F32, BF16 = jnp.float32, jnp.bfloat16


def split(value):
    high = value.astype(BF16)
    return high, (value - high.astype(F32)).astype(BF16)


def compact_kernel(round_ref, t_ref, v_ref, ij_ref, cd_ref, ab_ref, tc_ref, vc_ref):
    n_cd = cd_ref.shape[1]
    labels = cd_ref[...]
    member = lax.broadcasted_iota(jnp.int32, (G, n_cd), 0) == labels
    before = lax.broadcasted_iota(jnp.int32, (n_cd, n_cd), 0) < lax.broadcasted_iota(
        jnp.int32, (n_cd, n_cd), 1
    )
    below = jnp.dot(member.astype(BF16), before.astype(BF16), preferred_element_type=F32)
    rank = jnp.sum(jnp.where(member, below, 0.0), axis=0, keepdims=True).astype(jnp.int32)
    most = jnp.max(jnp.sum(member.astype(F32), axis=1, keepdims=True), axis=0, keepdims=True)
    place = rank - CAP * round_ref[0, 0]
    slot = jnp.where((place >= 0) & (place < CAP), labels * ROWS + place, -1)
    pick = (lax.broadcasted_iota(jnp.int32, (G * ROWS, n_cd), 0) == slot).astype(BF16)
    pick2 = jnp.concatenate([pick, pick], axis=1)

    def compacted(both, dims, column_labels, last_row):
        wide = lax.dot_general(pick2, both, (dims, ((), ())), preferred_element_type=F32)
        out = jnp.zeros((ROWS, wide.shape[1]), F32)
        for g in range(G):
            out = jnp.where(column_labels == g, wide[g * ROWS : (g + 1) * ROWS], out)
        row = lax.broadcasted_iota(jnp.int32, out.shape, 0)
        return jnp.where(row == CAP, last_row, out)

    ab = ab_ref[...]
    vc_ref[...] = compacted(
        jnp.concatenate(split(v_ref[...]), axis=0), ((1,), (0,)), ab, ab.astype(F32)
    )
    tc_ref[...] = compacted(
        jnp.concatenate(split(t_ref[...]), axis=1), ((1,), (1,)), ij_ref[...], most
    )


def compact(round_index, t, v, ij, cd, ab):
    vmem = pl.BlockSpec(memory_space=pltpu.VMEM)
    return pl.pallas_call(
        compact_kernel,
        out_shape=(
            jax.ShapeDtypeStruct((ROWS, t.shape[0]), F32),
            jax.ShapeDtypeStruct((ROWS, v.shape[1]), F32),
        ),
        in_specs=[pl.BlockSpec(memory_space=pltpu.SMEM)] + [vmem] * 5,
        out_specs=(vmem, vmem),
        compiler_params=pltpu.CompilerParams(vmem_limit_bytes=32 << 20),
        name="compact",
    )(round_index, t, v, ij[None, :], cd[None, :], ab[None, :])


def z_sends(quarter, d):
    up, down = (4, 3) if quarter % 2 == 0 else (3, 4)
    out = []
    if d < up:
        out.append(1)
    if d == 0 or 8 - d < down:
        out.append(-1)
    if d and d <= up and 8 - d <= down:
        raise ValueError
    if 0 < d <= up:
        return [s for s in out if s == 1]
    if d:
        return [s for s in out if s == -1]
    return out


def x_sends(quarter, dx):
    if dx == 0:
        return [1, -1]
    if dx == 1 and quarter % 2 == 0:
        return [1]
    if dx == 3 and quarter % 2 == 1:
        return [-1]
    return []


def gather_events():
    events = []
    for quarter in range(4):
        for d in range(8):
            for dx in range(4):
                x_hops = min(dx, 4 - dx)
                z_hops = min(d, 8 - d)
                if quarter < 2:
                    xs = x_sends(quarter, dx) if d == 0 else []
                    zs = z_sends(quarter, d)
                else:
                    xs = x_sends(quarter, dx)
                    zs = z_sends(quarter, d) if dx == 0 else []
                when = x_hops + z_hops
                events.append((when, z_hops if quarter < 2 else x_hops, quarter, d, dx, xs, zs))
    events.sort(key=lambda e: (e[0], e[1], e[3], e[4], e[2]))
    return [e[2:] for e in events]


EVENTS = gather_events()
N_SENDS = sum(len(e[3]) + len(e[4]) for e in EVENTS)


def gather_kernel(tc_ref, vc_ref, tg_ref, vg_ref, v_send, v_recv, y_send, t_send, t_recv, own_sem):
    occ, vir = lax.axis_index("occ"), lax.axis_index("vir")
    y_lo, z, x = occ // (NX * NZ), (occ // NX) % NZ, occ % NX
    y_hi, core = vir // 2, vir % 2
    u = (z + NZ - 4 * core) % NZ

    def at(y, z, x):
        return y * (NX * NZ) + z * NX + x

    def near_x(step):
        return (at(y_lo, z, (x + NX + step) % NX), vir)

    def near_z(step):
        return (at(y_lo, (z + NZ + step) % NZ, x), vir)

    other_y = (1 - y_lo) * (NX * NZ) + z * NX + x
    barrier = pltpu.get_barrier_semaphore()
    peers = [near_x(1), near_x(-1), near_z(1), near_z(-1)]
    peers += [(occ, (vir + k) % 4) for k in range(1, 4)]
    peers += [(other_y, k) for k in range(4)]
    for peer in peers:
        pl.semaphore_signal(barrier, inc=1, device_id=peer, device_id_type=MESH)
    pl.semaphore_wait(barrier, len(peers))

    block = (z % 4) * NX + x
    for k in range(2):
        target = (at(k, z, x), 2 * y_lo + z // 4)
        mine = (y_lo == k) & (vir == 2 * y_lo + z // 4)

        @pl.when(mine)
        def _():
            pltpu.make_async_copy(
                vc_ref, vg_ref.at[block, vir], v_recv.at[block * 4 + vir]
            ).start()

        @pl.when(jnp.logical_not(mine))
        def _():
            pltpu.make_async_remote_copy(
                src_ref=vc_ref,
                dst_ref=vg_ref.at[block, vir],
                send_sem=y_send.at[k],
                recv_sem=v_recv.at[block * 4 + vir],
                device_id=target,
                device_id_type=MESH,
            ).start()

    def t_copy(k):
        return pltpu.make_async_remote_copy(
            src_ref=tc_ref,
            dst_ref=tg_ref.at[vir],
            send_sem=t_send.at[k - 1],
            recv_sem=t_recv.at[k - 1],
            device_id=(occ, (vir + k) % 4),
            device_id_type=MESH,
        )

    own = pltpu.make_async_copy(tc_ref, tg_ref.at[vir], own_sem)

    def v_copy(quarter, zl, xs, peer, sem):
        here = vg_ref.at[zl * NX + xs, quarter]
        return pltpu.make_async_remote_copy(
            src_ref=here,
            dst_ref=here,
            send_sem=v_send.at[sem],
            recv_sem=v_recv.at[(zl * NX + xs) * 4 + quarter],
            device_id=peer,
            device_id_type=MESH,
        )

    def walk(act):
        sem = 0
        for quarter, d, dx, x_dirs, z_dirs in EVENTS:
            zl = (u + 8 - d) % 8
            xs = (x + NX - dx) % NX
            peers = [near_x(s) for s in x_dirs] + [near_z(s) for s in z_dirs]
            first = sem
            sem += len(peers)

            @pl.when(zl < 4)
            def _():
                act(quarter, zl, xs, peers, first)

    def receive_and_pass(quarter, zl, xs, peers, first):
        here = vg_ref.at[zl * NX + xs, quarter]
        pltpu.make_async_copy(here, here, v_recv.at[(zl * NX + xs) * 4 + quarter]).wait()
        for i, peer in enumerate(peers):
            v_copy(quarter, zl, xs, peer, first + i).start()

    def finish(quarter, zl, xs, peers, first):
        for i, peer in enumerate(peers):
            v_copy(quarter, zl, xs, peer, first + i).wait_send()

    own.start()
    for k in range(1, 4):
        t_copy(k).start()
    walk(receive_and_pass)
    walk(finish)
    own.wait()
    for k in range(1, 4):
        t_copy(k).wait()
    for k in range(2):
        mine = (y_lo == k) & (vir == 2 * y_lo + z // 4)

        @pl.when(jnp.logical_not(mine))
        def _():
            pltpu.make_async_remote_copy(
                src_ref=vc_ref,
                dst_ref=vg_ref.at[block, vir],
                send_sem=y_send.at[k],
                recv_sem=v_recv.at[block * 4 + vir],
                device_id=(at(k, z, x), 2 * y_lo + z // 4),
                device_id_type=MESH,
            ).wait_send()


def gather(tc, vc):
    anywhere = pl.BlockSpec(memory_space=pl.ANY)
    return pl.pallas_call(
        gather_kernel,
        out_shape=(
            jax.ShapeDtypeStruct((4,) + tc.shape, F32),
            jax.ShapeDtypeStruct((16, 4) + vc.shape, F32),
        ),
        in_specs=[anywhere, anywhere],
        out_specs=(anywhere, anywhere),
        scratch_shapes=[
            pltpu.SemaphoreType.DMA((N_SENDS,)),
            pltpu.SemaphoreType.DMA((64,)),
            pltpu.SemaphoreType.DMA((2,)),
            pltpu.SemaphoreType.DMA((3,)),
            pltpu.SemaphoreType.DMA((3,)),
            pltpu.SemaphoreType.DMA,
        ],
        compiler_params=pltpu.CompilerParams(collective_id=0, has_side_effects=True),
        name="gather",
    )(tc, vc)


def product_kernel(tg_ref, vg_ref, ij_ref, out_ref, rounds_ref, left, mask_col):
    slabs = tg_ref.shape[0]

    @pl.when(pl.program_id(0) == 0)
    def _():
        most = jnp.int32(0)
        for s in range(slabs):
            most = jnp.maximum(most, jnp.max(tg_ref[s, CAP:ROWS, :]).astype(jnp.int32))
        rounds_ref[0, 0] = (most + (CAP - 1)) // CAP
        parts = []
        row = lax.broadcasted_iota(jnp.int32, (ROWS, tg_ref.shape[2]), 0)
        for s in range(slabs):
            parts.append(jnp.where(row == CAP, 0.0, tg_ref[s]))
        high, low = split(jnp.concatenate(parts, axis=0).T)
        left[...] = jnp.concatenate([high, high, low], axis=1)
        mask_col[...] = jnp.broadcast_to(ij_ref[...].astype(F32), (128, ij_ref.shape[1])).T

    blocks = vg_ref.shape[0]
    value = jnp.concatenate(
        [
            jnp.concatenate([vg_ref[b, s] for s in range(slabs)], axis=0)
            for b in range(blocks)
        ],
        axis=1,
    )
    labels = jnp.concatenate([vg_ref[b, 0, CAP:ROWS, :] for b in range(blocks)], axis=1)
    high, low = split(value)
    right = jnp.concatenate([high, low, high], axis=0)
    total = jnp.dot(left[...], right, preferred_element_type=F32)
    same = jnp.concatenate([mask_col[...]] * blocks, axis=1) == labels
    out_ref[...] = jnp.where(same, total, 0.0)


def product(tg, vg, ij):
    slabs, rows, n_ij = tg.shape
    per_step = 2
    return pl.pallas_call(
        product_kernel,
        out_shape=(
            jax.ShapeDtypeStruct((n_ij, vg.shape[0] * 128), F32),
            jax.ShapeDtypeStruct((1, 1), jnp.int32),
        ),
        grid=(vg.shape[0] // per_step,),
        in_specs=[
            pl.BlockSpec(tg.shape, lambda i: (0, 0, 0)),
            pl.BlockSpec((per_step,) + vg.shape[1:], lambda i: (i, 0, 0, 0)),
            pl.BlockSpec((1, n_ij), lambda i: (0, 0)),
        ],
        out_specs=(
            pl.BlockSpec((n_ij, per_step * 128), lambda i: (0, i)),
            pl.BlockSpec((1, 1), lambda i: (0, 0), memory_space=pltpu.SMEM),
        ),
        scratch_shapes=[
            pltpu.VMEM((n_ij, 3 * slabs * rows), BF16),
            pltpu.VMEM((n_ij, 128), F32),
        ],
        compiler_params=pltpu.CompilerParams(vmem_limit_bytes=32 << 20),
        name="product",
    )(tg, vg, ij[None, :])


def per_device(amplitudes, integrals, ij_irrep, cd_irrep, ab_irrep):
    args = (amplitudes, integrals, ij_irrep, cd_irrep, ab_irrep)
    tc, vc = compact(jnp.zeros((1, 1), jnp.int32), *args)
    tg, vg = gather(tc, vc)
    ladder, rounds = product(tg, vg, ij_irrep)

    def more(state):
        return state[0] < rounds[0, 0]

    def one_round(state):
        index, total = state
        tc, vc = compact(index.reshape(1, 1), *args)
        tg = lax.all_gather(tc, "vir", axis=0)
        vg = lax.all_gather(lax.all_gather(vc, "occ", axis=0), "vir", axis=1)
        vg = lax.dynamic_slice_in_dim(vg, 16 * lax.axis_index("vir"), 16, axis=0)
        return index + 1, total + product(tg, vg, ij_irrep)[0]

    return lax.while_loop(more, one_round, (jnp.int32(1), ladder))[1]


def solution(mesh):
    in_specs = (P("occ", "vir"), P("vir", "occ"), P("occ"), P("vir"), P("occ"))
    out_specs = P("occ", "vir")
    return jax.shard_map(
        per_device, mesh=mesh, in_specs=in_specs, out_specs=out_specs, check_vma=False
    )
```

time: 529 us -> 73.5 us (0.14)
  the two profiles are of different devices: /device:TPU:1 before, /device:TPU:16 now
where the time goes in v1:
time: 73.5 us; the launch traced here: 73.2 us
  Pallas kernels  54.9 us (75%)
  between operations  13.5 us (18%)
  local copies, waits for them, and re-layouts  4.32 us (6%)
    pallas_call x1, Pallas kernels, gather(): pl.pallas_call(gather_kernel, out_shape=(jax.ShapeDtypeStruct((4,) + tc.s...  45 us
    pallas_call x1, Pallas kernels, product(): pl.pallas_call(product_kernel, out_shape=(jax.ShapeDtypeStruct((n_ij, vg....  6.82 us
    unnamed x18, local copies, waits for them, and re-layouts  4.32 us
    pallas_call x1, Pallas kernels, compact(): pl.pallas_call(compact_kernel, out_shape=(jax.ShapeDtypeStruct((ROWS, t.s...  3.02 us

profile of v1, /device:TPU:16, one launch (start us, length us, event | category | flops | bytes accessed | tf_op | source)
XLA Modules:
  0.0 73.2 jit_solution(12855407021362357355)
XLA Ops:
  6.5 0.0 copy-start.10
  6.5 0.0 copy-start.9
  6.5 0.0 copy-start.8
  6.5 0.0 copy-start.7
  6.5 0.0 copy-start.6
  6.5 3.0 %compact.2 = (f32[96,512]{1,0:T(8,128)S(1)}, f32[96,128]{1,0:T(8,128)S(1)}) custom-call(s32[1,1]{1,0:T(1,128)} %constant.6.clone.1.round_ref, f32[512,512]{1,0:T(8,128)} %t_ref.1, f32[512,128]{1,0:T(8,128)} %v_ref.1, s32[1,512]{1,0:T(1,128)} %bitcast.29, s32[1,512]{1,0:T(1,128)} %bitcast.33, s32[1,128]{1,0:T(1,128)} %bitcast.35), custom_call_target="tpu_custom_call" | custom-call | tf_op jit(solution)/shard_map/compact/pallas_call | solution.py:57
  9.6 0.0 copy-start.2
  9.6 0.7 copy-done.2
  10.3 0.0 copy-start.3
  10.3 0.6 copy-done.3
  10.9 45.0 %gather.1 = (f32[4,96,512]{2,1,0:T(8,128)}, f32[16,4,96,128]{3,2,1,0:T(8,128)}) custom-call(f32[96,512]{1,0:T(8,128)} %copy-done.2, f32[96,128]{1,0:T(8,128)} %copy-done.3), custom_call_target="tpu_custom_call" | custom-call | tf_op jit(solution)/shard_map/gather/pallas_call | solution.py:236
  55.9 0.0 copy-start
  55.9 1.9 %copy-done = f32[16,4,96,128]{3,2,1,0:T(8,128)S(1)} copy-done((f32[16,4,96,128]{3,2,1,0:T(8,128)S(1)}, f32[16,4,96,128]{3,2,1,0:T(8,128)}, u32[]{:S(2)}) %copy-start) | copy-done | bytes 3145752
  57.8 0.0 copy-start.1
  57.8 1.1 %copy-done.1 = f32[4,96,512]{2,1,0:T(8,128)S(1)} copy-done((f32[4,96,512]{2,1,0:T(8,128)S(1)}, f32[4,96,512]{2,1,0:T(8,128)}, u32[]{:S(2)}) %copy-start.1) | copy-done | bytes 786456
  58.9 6.8 %product.2 = (f32[512,2048]{1,0:T(8,128)}, s32[1,1]{1,0:T(1,128)}) custom-call(f32[4,96,512]{2,1,0:T(8,128)S(1)} %copy-done.1, f32[16,4,96,128]{3,2,1,0:T(8,128)S(1)} %copy-done, s32[1,512]{1,0:T(1,128)} %bitcast.30), custom_call_target="tpu_custom_call" | custom-call | tf_op jit(solution)/shard_map/product/pallas_call | solution.py:293
  65.7 0.0 copy-done.10
  65.7 0.0 copy-done.9
  65.7 0.0 copy-done.8
  65.7 0.0 copy-done.7
  65.8 0.0 copy-done.6
  65.8 0.6 while.10
Async XLA Ops:
  6.5 59.2 %copy-start.10 = (s32[128]{0:T(128)S(1)}, s32[128]{0:T(128)}, u32[]{:S(2)}) copy-start(s32[128]{0:T(128)} %param.11) | copy-start | bytes 1540
  6.5 59.2 %copy-start.9 = (s32[512]{0:T(512)S(1)}, s32[512]{0:T(512)}, u32[]{:S(2)}) copy-start(s32[512]{0:T(512)} %param.10) | copy-start | bytes 6148
  6.5 59.2 %copy-start.8 = (s32[512]{0:T(512)S(1)}, s32[512]{0:T(512)}, u32[]{:S(2)}) copy-start(s32[512]{0:T(512)} %param.9) | copy-start | bytes 6148
  6.5 59.2 %copy-start.7 = (f32[512,128]{1,0:T(8,128)S(1)}, f32[512,128]{1,0:T(8,128)}, u32[]{:S(2)}) copy-start(f32[512,128]{1,0:T(8,128)} %v_ref.1) | copy-start | bytes 786436
  6.5 59.2 %copy-start.6 = (f32[512,512]{1,0:T(8,128)S(1)}, f32[512,512]{1,0:T(8,128)}, u32[]{:S(2)}) copy-start(f32[512,512]{1,0:T(8,128)} %t_ref.1) | copy-start | bytes 3145732
  9.6 0.7 copy-start.2
  10.3 0.6 copy-start.3
  55.9 1.9 %copy-start = (f32[16,4,96,128]{3,2,1,0:T(8,128)S(1)}, f32[16,4,96,128]{3,2,1,0:T(8,128)}, u32[]{:S(2)}) copy-start(f32[16,4,96,128]{3,2,1,0:T(8,128)} %get-tuple-element.60.vg_ref) | copy-start | bytes 9437188
  57.8 1.1 %copy-start.1 = (f32[4,96,512]{2,1,0:T(8,128)S(1)}, f32[4,96,512]{2,1,0:T(8,128)}, u32[]{:S(2)}) copy-start(f32[4,96,512]{2,1,0:T(8,128)} %get-tuple-element.59.tg_ref) | copy-start | bytes 2359300

commit v2 on v1

--- a/solution.py
+++ b/solution.py
@@ -131,27 +131,38 @@
     def near_z(step):
         return (at(y_lo, (z + NZ + step) % NZ, x), vir)
 
-    other_y = (1 - y_lo) * (NX * NZ) + z * NX + x
+    owner = z // 4 == core
+    mine = owner & (y_lo == y_hi)
+    sibling, across = (occ, vir + 1 - 2 * core), (occ, (vir + 2) % 4)
+
     barrier = pltpu.get_barrier_semaphore()
-    peers = [near_x(1), near_x(-1), near_z(1), near_z(-1)]
-    peers += [(occ, (vir + k) % 4) for k in range(1, 4)]
-    peers += [(other_y, k) for k in range(4)]
-    for peer in peers:
+
+    def ready_for(peer):
         pl.semaphore_signal(barrier, inc=1, device_id=peer, device_id_type=MESH)
-    pl.semaphore_wait(barrier, len(peers))
+
+    for peer in (near_x(1), near_x(-1), sibling, across):
+        ready_for(peer)
+    pl.when(u != 0)(lambda: ready_for(near_z(-1)))
+    pl.when(u != 3)(lambda: ready_for(near_z(1)))
+    for k in range(4):
+        pl.when(owner & jnp.logical_not(mine & (vir == k)))(
+            lambda: ready_for((at(y_hi, z, x), k))
+        )
+    heard = 6 + (u != 7).astype(jnp.int32) + (u != 4).astype(jnp.int32)
+    pl.semaphore_wait(barrier, heard - mine.astype(jnp.int32))
 
     block = (z % 4) * NX + x
     for k in range(2):
         target = (at(k, z, x), 2 * y_lo + z // 4)
-        mine = (y_lo == k) & (vir == 2 * y_lo + z // 4)
-
-        @pl.when(mine)
+        here = mine & (y_lo == k)
+
+        @pl.when(here)
         def _():
             pltpu.make_async_copy(
                 vc_ref, vg_ref.at[block, vir], v_recv.at[block * 4 + vir]
             ).start()
 
-        @pl.when(jnp.logical_not(mine))
+        @pl.when(jnp.logical_not(here))
         def _():
             pltpu.make_async_remote_copy(
                 src_ref=vc_ref,
@@ -162,16 +173,20 @@
                 device_id_type=MESH,
             ).start()
 
-    def t_copy(k):
+    def t_copy(k, src, slab, peer):
         return pltpu.make_async_remote_copy(
-            src_ref=tc_ref,
-            dst_ref=tg_ref.at[vir],
-            send_sem=t_send.at[k - 1],
-            recv_sem=t_recv.at[k - 1],
-            device_id=(occ, (vir + k) % 4),
+            src_ref=src,
+            dst_ref=tg_ref.at[slab],
+            send_sem=t_send.at[k],
+            recv_sem=t_recv.at[k],
+            device_id=peer,
             device_id_type=MESH,
         )
 
+    far = (vir + 2) % 4
+    t_across = t_copy(0, tc_ref, vir, across)
+    t_near = t_copy(1, tc_ref, vir, sibling)
+    t_pass = t_copy(2, tg_ref.at[far], far, sibling)
     own = pltpu.make_async_copy(tc_ref, tg_ref.at[vir], own_sem)
 
     def v_copy(quarter, zl, xs, peer, sem):
@@ -187,7 +202,10 @@
 
     def walk(act):
         sem = 0
-        for quarter, d, dx, x_dirs, z_dirs in EVENTS:
+        for n, (quarter, d, dx, x_dirs, z_dirs) in enumerate(EVENTS):
+            if n == len(EVENTS) // 3 and act is receive_and_pass:
+                t_across.wait_recv()
+                t_pass.start()
             zl = (u + 8 - d) % 8
             xs = (x + NX - dx) % NX
             peers = [near_x(s) for s in x_dirs] + [near_z(s) for s in z_dirs]
@@ -209,17 +227,18 @@
             v_copy(quarter, zl, xs, peer, first + i).wait_send()
 
     own.start()
-    for k in range(1, 4):
-        t_copy(k).start()
+    t_across.start()
+    t_near.start()
     walk(receive_and_pass)
     walk(finish)
     own.wait()
-    for k in range(1, 4):
-        t_copy(k).wait()
+    t_near.wait()
+    t_across.wait_send()
+    t_pass.wait()
     for k in range(2):
-        mine = (y_lo == k) & (vir == 2 * y_lo + z // 4)
-
-        @pl.when(jnp.logical_not(mine))
+        here = mine & (y_lo == k)
+
+        @pl.when(jnp.logical_not(here))
         def _():
             pltpu.make_async_remote_copy(
                 src_ref=vc_ref,
@@ -249,7 +268,7 @@
             pltpu.SemaphoreType.DMA((3,)),
             pltpu.SemaphoreType.DMA,
         ],
-        compiler_params=pltpu.CompilerParams(collective_id=0, has_side_effects=True),
+        compiler_params=pltpu.CompilerParams(collective_id=0, has_side_effects=True, vmem_limit_bytes=8 << 20),
         name="gather",
     )(tc, vc)
 
@@ -327,9 +346,7 @@
     def one_round(state):
         index, total = state
         tc, vc = compact(index.reshape(1, 1), *args)
-        tg = lax.all_gather(tc, "vir", axis=0)
-        vg = lax.all_gather(lax.all_gather(vc, "occ", axis=0), "vir", axis=1)
-        vg = lax.dynamic_slice_in_dim(vg, 16 * lax.axis_index("vir"), 16, axis=0)
+        tg, vg = gather(tc, vc)
         return index + 1, total + product(tg, vg, ij_irrep)[0]
 
     return lax.while_loop(more, one_round, (jnp.int32(1), ladder))[1]

time: 73.5 us -> 46.6 us (0.63)
  the two profiles are of different devices: /device:TPU:16 before, /device:TPU:1 now
where the time goes in v2:
time: 46.6 us; the launch traced here: 46.2 us
  Pallas kernels  45.6 us (98%)
  loops' own time  0.57 us (1%)
    pallas_call x1, Pallas kernels, gather(): pl.pallas_call(gather_kernel, out_shape=(jax.ShapeDtypeStruct((4,) + tc.s...  35.7 us
    pallas_call x1, Pallas kernels, product(): pl.pallas_call(product_kernel, out_shape=(jax.ShapeDtypeStruct((n_ij, vg....  6.85 us
    pallas_call x1, Pallas kernels, compact(): pl.pallas_call(compact_kernel, out_shape=(jax.ShapeDtypeStruct((ROWS, t.s...  3.02 us

profile of v2, /device:TPU:1, one launch (start us, length us, event | category | flops | bytes accessed | tf_op | source)
XLA Modules:
  0.0 46.2 jit_solution(13633784948230299084)
XLA Ops:
  0.0 0.0 copy-start.6
  0.0 0.0 copy-start.5
  0.0 0.0 copy-start.4
  0.0 0.0 copy-start.3
  0.0 0.0 copy-start.2
  0.0 3.0 %compact.2 = (f32[96,512]{1,0:T(8,128)S(1)}, f32[96,128]{1,0:T(8,128)S(1)}) custom-call(s32[1,1]{1,0:T(1,128)} %constant.2.clone.1.round_ref, f32[512,512]{1,0:T(8,128)} %t_ref.1, f32[512,128]{1,0:T(8,128)} %v_ref.1, s32[1,512]{1,0:T(1,128)} %bitcast.17, s32[1,512]{1,0:T(1,128)} %bitcast.21, s32[1,128]{1,0:T(1,128)} %bitcast.23), custom_call_target="tpu_custom_call" | custom-call | tf_op jit(solution)/shard_map/compact/pallas_call | solution.py:57
  3.1 35.7 %gather.2 = (f32[4,96,512]{2,1,0:T(8,128)S(1)}, f32[16,4,96,128]{3,2,1,0:T(8,128)S(1)}) custom-call(f32[96,512]{1,0:T(8,128)S(1)} %get-tuple-element.59.tc_ref, f32[96,128]{1,0:T(8,128)S(1)} %get-tuple-element.60.vc_ref), custom_call_target="tpu_custom_call" | custom-call | tf_op jit(solution)/shard_map/gather/pallas_call | solution.py:255
  38.8 6.9 %product.2 = (f32[512,2048]{1,0:T(8,128)}, s32[1,1]{1,0:T(1,128)}) custom-call(f32[4,96,512]{2,1,0:T(8,128)S(1)} %get-tuple-element.61.tg_ref, f32[16,4,96,128]{3,2,1,0:T(8,128)S(1)} %get-tuple-element.62.vg_ref, s32[1,512]{1,0:T(1,128)} %bitcast.18), custom_call_target="tpu_custom_call" | custom-call | tf_op jit(solution)/shard_map/product/pallas_call | solution.py:312
  45.6 0.0 copy-done.6
  45.6 0.0 copy-done.5
  45.6 0.0 copy-done.4
  45.6 0.0 copy-done.3
  45.7 0.0 copy-done.2
  45.7 0.6 %while.10 = (s32[]{:T(128)}, f32[512,2048]{1,0:T(8,128)}, s32[1,1]{1,0:T(1,128)}, s32[512]{0:T(512)S(1)}, s32[512]{0:T(512)S(1)}, /*index=5*/s32[128]{0:T(128)S(...) while((s32[]{:T(128)}, f32[512,2048]{1,0:T(8,128)}, s32[1,1]{1,0:T(1,128)}, s32[512]{0:T(512)S(1)}, ...), condition=%wide.region_1.0_spmd, body=%wide.region_0.0_spmd.sunk | while | flops 1048578 | bytes 46137500 | solution.py:352
Async XLA Ops:
  0.0 45.6 %copy-start.6 = (s32[128]{0:T(128)S(1)}, s32[128]{0:T(128)}, u32[]{:S(2)}) copy-start(s32[128]{0:T(128)} %param.11) | copy-start | bytes 1540
  0.0 45.6 %copy-start.5 = (s32[512]{0:T(512)S(1)}, s32[512]{0:T(512)}, u32[]{:S(2)}) copy-start(s32[512]{0:T(512)} %param.10) | copy-start | bytes 6148
  0.0 45.6 %copy-start.4 = (s32[512]{0:T(512)S(1)}, s32[512]{0:T(512)}, u32[]{:S(2)}) copy-start(s32[512]{0:T(512)} %param.9) | copy-start | bytes 6148
  0.0 45.6 %copy-start.3 = (f32[512,128]{1,0:T(8,128)S(1)}, f32[512,128]{1,0:T(8,128)}, u32[]{:S(2)}) copy-start(f32[512,128]{1,0:T(8,128)} %v_ref.1) | copy-start | bytes 786436
  0.0 45.6 %copy-start.2 = (f32[512,512]{1,0:T(8,128)S(1)}, f32[512,512]{1,0:T(8,128)}, u32[]{:S(2)}) copy-start(f32[512,512]{1,0:T(8,128)} %t_ref.1) | copy-start | bytes 3145732

commit v3 on v2

v3 whole, which is shorter than its diff:
```python
import functools

import jax
import jax.numpy as jnp
from jax import lax
from jax.experimental import pallas as pl
from jax.experimental.pallas import tpu as pltpu
from jax.sharding import PartitionSpec as P

MESH = pl.DeviceIdType.MESH
G = 8
CAP = 95
ROWS = CAP + 1
NX, NZ = 4, 8
F32, BF16 = jnp.float32, jnp.bfloat16


def split(value):
    high = value.astype(BF16)
    return high, (value - high.astype(F32)).astype(BF16)


def picker(round_index, labels):
    n_cd = labels.shape[1]
    member = lax.broadcasted_iota(jnp.int32, (G, n_cd), 0) == labels
    before = lax.broadcasted_iota(jnp.int32, (n_cd, n_cd), 0) < lax.broadcasted_iota(
        jnp.int32, (n_cd, n_cd), 1
    )
    below = jnp.dot(member.astype(BF16), before.astype(BF16), preferred_element_type=F32)
    rank = jnp.sum(jnp.where(member, below, 0.0), axis=0, keepdims=True).astype(jnp.int32)
    most = jnp.max(jnp.sum(member.astype(F32), axis=1, keepdims=True), axis=0, keepdims=True)
    place = rank - CAP * round_index
    slot = jnp.where((place >= 0) & (place < CAP), labels * ROWS + place, -1)
    pick = (lax.broadcasted_iota(jnp.int32, (G * ROWS, n_cd), 0) == slot).astype(BF16)
    return jnp.concatenate([pick, pick], axis=1), most


def compacted(pick2, both, dims, column_labels, last_row):
    wide = lax.dot_general(pick2, both, (dims, ((), ())), preferred_element_type=F32)
    out = jnp.zeros((ROWS, wide.shape[1]), F32)
    for g in range(G):
        out = jnp.where(column_labels == g, wide[g * ROWS : (g + 1) * ROWS], out)
    row = lax.broadcasted_iota(jnp.int32, out.shape, 0)
    return jnp.where(row == CAP, last_row, out)


def z_sends(quarter, d):
    up, down = (4, 3) if quarter % 2 == 0 else (3, 4)
    out = []
    if d < up:
        out.append(1)
    if d == 0 or 8 - d < down:
        out.append(-1)
    if d and d <= up and 8 - d <= down:
        raise ValueError
    if 0 < d <= up:
        return [s for s in out if s == 1]
    if d:
        return [s for s in out if s == -1]
    return out


def x_sends(quarter, dx):
    if dx == 0:
        return [1, -1]
    if dx == 1 and quarter % 2 == 0:
        return [1]
    if dx == 3 and quarter % 2 == 1:
        return [-1]
    return []


def spread_events():
    events = []
    for quarter in range(4):
        for d in range(8):
            for dx in range(4):
                x_hops = min(dx, 4 - dx)
                z_hops = min(d, 8 - d)
                if quarter < 2:
                    xs = x_sends(quarter, dx) if d == 0 else []
                    zs = z_sends(quarter, d)
                else:
                    xs = x_sends(quarter, dx)
                    zs = z_sends(quarter, d) if dx == 0 else []
                when = x_hops + z_hops
                late = z_hops if quarter < 2 else x_hops
                events.append((when, late, d, dx, quarter, xs, zs))
    return sorted(events)


EVENTS = spread_events()
N_SENDS = sum(len(e[5]) + len(e[6]) for e in EVENTS)
LAST_HOPS = max(e[0] for e in EVENTS)
SLABS = 4
QUARTERS = ((0, 80), (80, 80), (160, 112), (272, 112))


def spread_kernel(
    round_ref, t_hbm, v_hbm, ij_ref, cd_ref, ab_ref, vg_ref, left_ref, mask_ref, rounds_ref,
    t_buf, v_buf, vc_ref, tg_ref, pick_ref, v_send, v_recv, y_send, t_send, t_recv, in_sem,
):
    t_in = pltpu.make_async_copy(t_hbm, t_buf, in_sem.at[0])
    v_in = pltpu.make_async_copy(v_hbm, v_buf, in_sem.at[1])
    v_in.start()
    t_in.start()
    occ, vir = lax.axis_index("occ"), lax.axis_index("vir")
    y_lo, z, x = occ // (NX * NZ), (occ // NX) % NZ, occ % NX
    y_hi, core = vir // 2, vir % 2
    u = (z + NZ - 4 * core) % NZ

    def at(y, z, x):
        return y * (NX * NZ) + z * NX + x

    def near_x(step):
        return (at(y_lo, z, (x + NX + step) % NX), vir)

    def near_z(step):
        return (at(y_lo, (z + NZ + step) % NZ, x), vir)

    owner = z // 4 == core
    mine = owner & (y_lo == y_hi)
    sibling, across = (occ, vir + 1 - 2 * core), (occ, (vir + 2) % 4)

    barrier = pltpu.get_barrier_semaphore()

    def ready_for(peer):
        pl.semaphore_signal(barrier, inc=1, device_id=peer, device_id_type=MESH)

    for peer in (near_x(1), near_x(-1), sibling, across):
        ready_for(peer)
    pl.when(u != 0)(lambda: ready_for(near_z(-1)))
    pl.when(u != 3)(lambda: ready_for(near_z(1)))
    for k in range(4):
        pl.when(owner & jnp.logical_not(mine & (vir == k)))(
            lambda: ready_for((at(y_hi, z, x), k))
        )
    heard = 6 + (u != 7).astype(jnp.int32) + (u != 4).astype(jnp.int32)

    pick2, most = picker(round_ref[0, 0], cd_ref[...])
    pick_ref[...] = pick2
    ab = ab_ref[...]
    v_in.wait()
    both = jnp.concatenate(split(v_buf[...]), axis=0)
    vc_ref[...] = compacted(pick2, both, ((1,), (0,)), ab, ab.astype(F32))
    pl.semaphore_wait(barrier, heard - mine.astype(jnp.int32))

    block = (z % 4) * NX + x
    for k in range(2):
        target = (at(k, z, x), 2 * y_lo + z // 4)
        here = mine & (y_lo == k)

        @pl.when(here)
        def _():
            pltpu.make_async_copy(
                vc_ref, vg_ref.at[block, pl.ds(vir * ROWS, ROWS)], v_recv.at[block * 4 + vir]
            ).start()

        @pl.when(jnp.logical_not(here))
        def _():
            pltpu.make_async_remote_copy(
                src_ref=vc_ref,
                dst_ref=vg_ref.at[block, pl.ds(vir * ROWS, ROWS)],
                send_sem=y_send.at[k],
                recv_sem=v_recv.at[block * 4 + vir],
                device_id=target,
                device_id_type=MESH,
            ).start()

    def t_copy(k, src, slab, peer):
        return pltpu.make_async_remote_copy(
            src_ref=src,
            dst_ref=tg_ref.at[slab],
            send_sem=t_send.at[k],
            recv_sem=t_recv.at[k],
            device_id=peer,
            device_id_type=MESH,
        )

    far = (vir + 2) % 4
    t_across = t_copy(0, tg_ref.at[vir], vir, across)
    t_near = t_copy(1, tg_ref.at[vir], vir, sibling)
    t_pass = t_copy(2, tg_ref.at[far], far, sibling)
    t_in.wait()
    both = jnp.concatenate(split(t_buf[...]), axis=1)
    tg_ref[vir] = compacted(pick_ref[...], both, ((1,), (1,)), ij_ref[...], most)

    def v_copy(quarter, zl, xs, peer, sem):
        here = vg_ref.at[zl * NX + xs, pl.ds(*QUARTERS[quarter])]
        return pltpu.make_async_remote_copy(
            src_ref=here,
            dst_ref=here,
            send_sem=v_send.at[sem],
            recv_sem=v_recv.at[(zl * NX + xs) * 4 + quarter],
            device_id=peer,
            device_id_type=MESH,
        )

    def walk(act, after_hops):
        sem = 0
        for n, (hops, _, d, dx, quarter, x_dirs, z_dirs) in enumerate(EVENTS):
            if n and hops > EVENTS[n - 1][0]:
                after_hops(EVENTS[n - 1][0])
            zl = (u + 8 - d) % 8
            xs = (x + NX - dx) % NX
            peers = [near_x(s) for s in x_dirs] + [near_z(s) for s in z_dirs]
            first = sem
            sem += len(peers)

            @pl.when(zl < 4)
            def _():
                act(quarter, zl, xs, peers, first, d == 0 and dx == 0)

    def receive_and_pass(quarter, zl, xs, peers, first, own):
        start, size = (quarter * ROWS, ROWS) if own else QUARTERS[quarter]
        here = vg_ref.at[zl * NX + xs, pl.ds(start, size)]
        pltpu.make_async_copy(here, here, v_recv.at[(zl * NX + xs) * 4 + quarter]).wait()
        for i, peer in enumerate(peers):
            v_copy(quarter, zl, xs, peer, first + i).start()

    def finish(quarter, zl, xs, peers, first, own):
        for i, peer in enumerate(peers):
            v_copy(quarter, zl, xs, peer, first + i).wait_send()

    def between(hops):
        if hops == 2:
            t_across.wait_recv()
            t_pass.start()
        if hops == LAST_HOPS - 1:
            t_near.wait_recv()
            t_pass.wait_recv()
            most = jnp.float32(0)
            for s in range(SLABS):
                most = jnp.maximum(most, jnp.max(tg_ref[s, CAP:ROWS, :]))
            rounds_ref[0, 0] = (most.astype(jnp.int32) + (CAP - 1)) // CAP
            row = lax.broadcasted_iota(jnp.int32, tg_ref.shape[1:], 0)
            parts = [jnp.where(row == CAP, 0.0, tg_ref[s]) for s in range(SLABS)]
            high, low = split(jnp.concatenate(parts, axis=0).T)
            left_ref[...] = jnp.concatenate([high, high, low], axis=1)
            labels = ij_ref[...].astype(F32)
            mask_ref[...] = jnp.broadcast_to(labels, (128, labels.shape[1])).T

    t_across.start()
    t_near.start()
    walk(receive_and_pass, between)
    walk(finish, lambda hops: None)
    for copy in (t_across, t_near, t_pass):
        copy.wait_send()
    for k in range(2):
        here = mine & (y_lo == k)

        @pl.when(jnp.logical_not(here))
        def _():
            pltpu.make_async_remote_copy(
                src_ref=vc_ref,
                dst_ref=vg_ref.at[block, pl.ds(vir * ROWS, ROWS)],
                send_sem=y_send.at[k],
                recv_sem=v_recv.at[block * 4 + vir],
                device_id=(at(k, z, x), 2 * y_lo + z // 4),
                device_id_type=MESH,
            ).wait_send()


def spread(round_index, t, v, ij, cd, ab):
    n_ij, n_cd = t.shape
    anywhere = pl.BlockSpec(memory_space=pl.ANY)
    vmem = pl.BlockSpec(memory_space=pltpu.VMEM)
    smem = pl.BlockSpec(memory_space=pltpu.SMEM)
    return pl.pallas_call(
        spread_kernel,
        out_shape=(
            jax.ShapeDtypeStruct((16, SLABS * ROWS, v.shape[1]), F32),
            jax.ShapeDtypeStruct((n_ij, 3 * SLABS * ROWS), BF16),
            jax.ShapeDtypeStruct((n_ij, 128), F32),
            jax.ShapeDtypeStruct((1, 1), jnp.int32),
        ),
        in_specs=[smem, anywhere, anywhere, vmem, vmem, vmem],
        out_specs=(anywhere, vmem, vmem, smem),
        scratch_shapes=[
            pltpu.VMEM(t.shape, F32),
            pltpu.VMEM(v.shape, F32),
            pltpu.VMEM((ROWS, v.shape[1]), F32),
            pltpu.VMEM((SLABS, ROWS, n_ij), F32),
            pltpu.VMEM((G * ROWS, 2 * n_cd), BF16),
            pltpu.SemaphoreType.DMA((N_SENDS,)),
            pltpu.SemaphoreType.DMA((64,)),
            pltpu.SemaphoreType.DMA((2,)),
            pltpu.SemaphoreType.DMA((3,)),
            pltpu.SemaphoreType.DMA((3,)),
            pltpu.SemaphoreType.DMA((2,)),
        ],
        compiler_params=pltpu.CompilerParams(
            collective_id=0, has_side_effects=True, vmem_limit_bytes=24 << 20
        ),
        name="spread",
    )(round_index, t, v, ij[None, :], cd[None, :], ab[None, :])


def product_kernel(left_ref, vg_ref, mask_ref, out_ref):
    blocks = vg_ref.shape[0]
    value = jnp.concatenate([vg_ref[b] for b in range(blocks)], axis=1)
    labels = jnp.concatenate([vg_ref[b, CAP:ROWS, :] for b in range(blocks)], axis=1)
    high, low = split(value)
    right = jnp.concatenate([high, low, high], axis=0)
    total = jnp.dot(left_ref[...], right, preferred_element_type=F32)
    same = jnp.concatenate([mask_ref[...]] * blocks, axis=1) == labels
    out_ref[...] = jnp.where(same, total, 0.0)


def product(left, vg, mask):
    n_ij, per_step = left.shape[0], 2
    return pl.pallas_call(
        product_kernel,
        out_shape=jax.ShapeDtypeStruct((n_ij, vg.shape[0] * 128), F32),
        grid=(vg.shape[0] // per_step,),
        in_specs=[
            pl.BlockSpec(left.shape, lambda i: (0, 0)),
            pl.BlockSpec((per_step,) + vg.shape[1:], lambda i: (i, 0, 0)),
            pl.BlockSpec(mask.shape, lambda i: (0, 0)),
        ],
        out_specs=pl.BlockSpec((n_ij, per_step * 128), lambda i: (0, i)),
        compiler_params=pltpu.CompilerParams(vmem_limit_bytes=24 << 20),
        name="product",
    )(left, vg, mask)


def per_device(*args):
    def one_round(index):
        vg, left, mask, rounds = spread(index.reshape(1, 1), *args)
        return product(left, vg, mask), rounds

    ladder, rounds = one_round(jnp.int32(0))

    def more(state):
        return state[0] < rounds[0, 0]

    def next_round(state):
        index, total = state
        return index + 1, total + one_round(index)[0]

    return lax.while_loop(more, next_round, (jnp.int32(1), ladder))[1]


def solution(mesh):
    in_specs = (P("occ", "vir"), P("vir", "occ"), P("occ"), P("vir"), P("occ"))
    out_specs = P("occ", "vir")
    return jax.shard_map(
        per_device, mesh=mesh, in_specs=in_specs, out_specs=out_specs, check_vma=False
    )
```

time: 46.6 us -> 44.2 us (0.948)
  Pallas kernels: 45.6 us -> 43.3 us
    pallas_call x3 -> x2, Pallas kernels: 45.6 us -> 43.3 us  [the longest x1 37.5 us: spread(): pl.pallas_call(spread_kernel, out_shape=(jax.ShapeDtypeStruct((16, SLABS...]
where the time goes in v3:
time: 44.2 us; the launch traced here: 44 us
  Pallas kernels  43.3 us (98%)
  loops' own time  0.63 us (1%)
    pallas_call x1, Pallas kernels, spread(): pl.pallas_call(spread_kernel, out_shape=(jax.ShapeDtypeStruct((16, SLABS...  37.5 us
    pallas_call x1, Pallas kernels, product(): pl.pallas_call(product_kernel, out_shape=jax.ShapeDtypeStruct((n_ij, vg.s...  5.78 us

profile of v3, /device:TPU:1, one launch (start us, length us, event | category | flops | bytes accessed | tf_op | source)
XLA Modules:
  0.0 44.0 jit_solution(3164127231501804694)
XLA Ops:
  0.0 37.5 %spread.2 = (f32[16,384,128]{2,1,0:T(8,128)S(1)}, bf16[512,1152]{1,0:T(8,128)(2,1)S(1)}, f32[512,128]{1,0:T(8,128)S(1)}, s32[1,1]{1,0:T(1,128)}) custom-call(s32[1,1]{1,0:T(1,128)} %constant.2.clone.1.round_ref, f32[512,512]{1,0:T(8,128)} %t_hbm.1, f32[512,128]{1,0:T(8,128)} %v_hbm.1, s32[1,512]{1,0:T(1,128)} %bitcast.17, s32[1,512]{1,0:T(1,128)} %bitcast.19, ...), custom_call_target="tpu_custom_call" | custom-call | tf_op jit(solution)/shard_map/spread/pallas_call | solution.py:269
  37.5 0.0 copy-start.2
  37.5 0.0 copy-start.3
  37.5 0.0 copy-start.4
  37.6 0.0 copy-start.5
  37.6 0.0 copy-start.6
  37.6 5.8 %product.2 = f32[512,2048]{1,0:T(8,128)} custom-call(bf16[512,1152]{1,0:T(8,128)(2,1)S(1)} %get-tuple-element.55.left_ref, f32[16,384,128]{2,1,0:T(8,128)S(1)} %get-tuple-element.56.vg_ref, f32[512,128]{1,0:T(8,128)S(1)} %get-tuple-element.57.mask_ref), custom_call_target="tpu_custom_call" | custom-call | tf_op jit(solution)/shard_map/product/pallas_call | solution.py:312
  43.4 0.0 copy-done.2
  43.4 0.0 copy-done.3
  43.4 0.0 copy-done.4
  43.4 0.0 copy-done.5
  43.4 0.0 copy-done.6
  43.4 0.6 %while.10 = (s32[]{:T(128)}, f32[512,2048]{1,0:T(8,128)}, s32[1,1]{1,0:T(1,128)}, s32[512]{0:T(512)S(1)}, s32[512]{0:T(512)S(1)}, /*index=5*/s32[128]{0:T(128)S(...) while((s32[]{:T(128)}, f32[512,2048]{1,0:T(8,128)}, s32[1,1]{1,0:T(1,128)}, s32[512]{0:T(512)S(1)}, ...), condition=%wide.region_1.0_spmd, body=%wide.region_0.0_spmd.sunk | while | flops 1048578 | bytes 46137500 | solution.py:341
Async XLA Ops:
  37.5 5.8 %copy-start.2 = (f32[512,512]{1,0:T(8,128)S(1)}, f32[512,512]{1,0:T(8,128)}, u32[]{:S(2)}) copy-start(f32[512,512]{1,0:T(8,128)} %t_hbm.1) | copy-start | bytes 3145732
  37.5 5.8 %copy-start.3 = (f32[512,128]{1,0:T(8,128)S(1)}, f32[512,128]{1,0:T(8,128)}, u32[]{:S(2)}) copy-start(f32[512,128]{1,0:T(8,128)} %v_hbm.1) | copy-start | bytes 786436
  37.5 5.8 %copy-start.4 = (s32[512]{0:T(512)S(1)}, s32[512]{0:T(512)}, u32[]{:S(2)}) copy-start(s32[512]{0:T(512)} %param.9) | copy-start | bytes 6148
  37.6 5.8 %copy-start.5 = (s32[512]{0:T(512)S(1)}, s32[512]{0:T(512)}, u32[]{:S(2)}) copy-start(s32[512]{0:T(512)} %param.10) | copy-start | bytes 6148
  37.6 5.8 %copy-start.6 = (s32[128]{0:T(128)S(1)}, s32[128]{0:T(128)}, u32[]{:S(2)}) copy-start(s32[128]{0:T(128)} %param.11) | copy-start | bytes 1540

commit v4 on v3

v4 whole, which is shorter than its diff:
```python
import functools

import jax
import jax.numpy as jnp
from jax import lax
from jax.experimental import pallas as pl
from jax.experimental.pallas import tpu as pltpu
from jax.sharding import PartitionSpec as P

MESH = pl.DeviceIdType.MESH
G = 8
CAP = 95
ROWS = CAP + 1
NX, NZ = 4, 8
F32, BF16 = jnp.float32, jnp.bfloat16


def split(value):
    high = value.astype(BF16)
    return high, (value - high.astype(F32)).astype(BF16)


def picker(round_index, labels):
    n_cd = labels.shape[1]
    member = lax.broadcasted_iota(jnp.int32, (G, n_cd), 0) == labels
    before = lax.broadcasted_iota(jnp.int32, (n_cd, n_cd), 0) < lax.broadcasted_iota(
        jnp.int32, (n_cd, n_cd), 1
    )
    below = jnp.dot(member.astype(BF16), before.astype(BF16), preferred_element_type=F32)
    rank = jnp.sum(jnp.where(member, below, 0.0), axis=0, keepdims=True).astype(jnp.int32)
    most = jnp.max(jnp.sum(member.astype(F32), axis=1, keepdims=True), axis=0, keepdims=True)
    place = rank - CAP * round_index
    slot = jnp.where((place >= 0) & (place < CAP), labels * ROWS + place, -1)
    pick = (lax.broadcasted_iota(jnp.int32, (G * ROWS, n_cd), 0) == slot).astype(BF16)
    return jnp.concatenate([pick, pick], axis=1), most


def compacted(pick2, both, dims, column_labels, last_row):
    wide = lax.dot_general(pick2, both, (dims, ((), ())), preferred_element_type=F32)
    out = jnp.zeros((ROWS, wide.shape[1]), F32)
    for g in range(G):
        out = jnp.where(column_labels == g, wide[g * ROWS : (g + 1) * ROWS], out)
    row = lax.broadcasted_iota(jnp.int32, out.shape, 0)
    return jnp.where(row == CAP, last_row, out)


SLABS = 4
PARTS = ((0, 80), (80, 80), (160, 112), (272, 112))
PARENTS = (
    (-1, 0, 1, 0, 0, 1, 2, 3, 4, 5, 6, 7, 8, 9, 10, 11,
     12, 13, 14, 15, 24, 25, 26, 27, 28, 29, 30, 31, 0, 1, 2, 3),
    (-1, 0, 3, 0, 0, 1, 2, 3, 4, 5, 6, 7, 8, 9, 10, 11,
     20, 21, 22, 23, 24, 25, 26, 27, 28, 29, 30, 31, 0, 1, 2, 3),
    (-1, 0, 1, 0, 0, 4, 5, 4, 4, 8, 9, 8, 8, 12, 13, 12,
     12, 16, 17, 16, 24, 20, 21, 20, 28, 24, 25, 24, 0, 28, 29, 28),
    (-1, 0, 3, 0, 0, 4, 7, 4, 4, 8, 11, 8, 8, 12, 15, 12,
     20, 16, 19, 16, 24, 20, 23, 20, 28, 24, 27, 24, 0, 28, 31, 28),
)
ORDER = (
    0, 32, 64, 96, 1, 33, 3, 35, 68, 100, 92, 124, 65, 97, 67, 99, 4, 36, 28, 60, 2, 34, 72, 104,
    88, 120, 5, 37, 69, 101, 7, 39, 71, 103, 29, 61, 93, 125, 31, 63, 95, 127, 66, 98, 8, 40, 24,
    56, 76, 108, 84, 116, 6, 38, 73, 105, 75, 107, 89, 121, 91, 123, 30, 62, 70, 102, 9, 41, 11,
    43, 25, 57, 27, 59, 94, 126, 12, 44, 20, 52, 80, 112, 77, 109, 79, 111, 85, 117, 87, 119, 10,
    42, 74, 106, 26, 58, 90, 122, 13, 45, 15, 47, 21, 53, 23, 55, 16, 48, 81, 113, 83, 115, 78,
    110, 86, 118, 14, 46, 22, 54, 17, 49, 19, 51, 82, 114, 18, 50,
)


def spread_plan():
    events, seen = [], set()
    children = [[[] for _ in range(32)] for _ in PARTS]
    for part, parents in enumerate(PARENTS):
        for child, parent in enumerate(parents):
            if parent >= 0:
                children[part][parent].append(child)

    def height(part, node):
        return max([1 + height(part, c) for c in children[part][node]], default=0)

    for item in ORDER:
        part, node = item // 32, item % 32
        below = sorted(children[part][node], key=lambda c: -height(part, c))
        if node:
            arrivals = [part]
        else:
            start, size = PARTS[part]
            spans = range(start // ROWS, (start + size - 1) // ROWS + 1)
            arrivals = [slab for slab in spans if slab not in seen]
            seen.update(arrivals)
        if below:
            events.append((part, node // 4, node % 4, below, arrivals))
    leaves = [[not c for c in nodes] for nodes in children]
    return events, leaves


EVENTS, LEAVES = spread_plan()


SENT = [
    [sum(len(e[3]) for e in EVENTS if e[:2] == (part, dz)) for dz in range(NZ)]
    for part in range(len(PARTS))
]


STEPS = {}
for _part, _dz, _dx, _below, _ in EVENTS:
    for _c in _below:
        _step = ((_c // 4 - _dz) % NZ, (_c % 4 - _dx) % NX)
        STEPS.setdefault(_step, set()).update((_dz + zl) % NZ for zl in range(4))


def among(u, values):
    return functools.reduce(jnp.logical_or, [u == v for v in sorted(values)])


def spread_kernel(
    round_ref, t_hbm, v_hbm, ij_ref, cd_ref, ab_ref, vg_ref, left_ref, mask_ref, rounds_ref,
    t_buf, v_buf, vc_ref, tg_ref, pick_ref, v_send, v_recv, leaf_recv, y_send, t_send, t_recv, in_sem,
):
    t_in = pltpu.make_async_copy(t_hbm, t_buf, in_sem.at[0])
    v_in = pltpu.make_async_copy(v_hbm, v_buf, in_sem.at[1])
    v_in.start()
    t_in.start()
    occ, vir = lax.axis_index("occ"), lax.axis_index("vir")
    y_lo, z, x = occ // (NX * NZ), (occ // NX) % NZ, occ % NX
    y_hi, core = vir // 2, vir % 2
    u = (z + NZ - 4 * core) % NZ

    def at(y, z, x):
        return y * (NX * NZ) + z * NX + x

    def away(dz, dx):
        return (at(y_lo, (z + NZ + dz) % NZ, (x + NX + dx) % NX), vir)

    owner = z // 4 == core
    mine = owner & (y_lo == y_hi)
    sibling, across = (occ, vir + 1 - 2 * core), (occ, (vir + 2) % 4)

    barrier = pltpu.get_barrier_semaphore()

    def ready_for(peer):
        pl.semaphore_signal(barrier, inc=1, device_id=peer, device_id_type=MESH)

    for peer in (sibling, across):
        ready_for(peer)
    heard = 4 - mine.astype(jnp.int32)
    for (dz, dx), senders in STEPS.items():
        source = (u + NZ - dz) % NZ
        pl.when(among(source, senders))(lambda: ready_for(away(-dz, -dx)))
        heard += among(u, senders).astype(jnp.int32)
    for k in range(4):
        pl.when(owner & jnp.logical_not(mine & (vir == k)))(
            lambda: ready_for((at(y_hi, z, x), k))
        )

    pick2, most = picker(round_ref[0, 0], cd_ref[...])
    pick_ref[...] = pick2
    ab = ab_ref[...]
    v_in.wait()
    both = jnp.concatenate(split(v_buf[...]), axis=0)
    vc_ref[...] = compacted(pick2, both, ((1,), (0,)), ab, ab.astype(F32))
    pl.semaphore_wait(barrier, heard)

    block = (z % 4) * NX + x
    for k in range(2):
        target = (at(k, z, x), 2 * y_lo + z // 4)
        here = mine & (y_lo == k)

        @pl.when(here)
        def _():
            pltpu.make_async_copy(
                vc_ref, vg_ref.at[block, pl.ds(vir * ROWS, ROWS)], v_recv.at[block * 4 + vir]
            ).start()

        @pl.when(jnp.logical_not(here))
        def _():
            pltpu.make_async_remote_copy(
                src_ref=vc_ref,
                dst_ref=vg_ref.at[block, pl.ds(vir * ROWS, ROWS)],
                send_sem=y_send.at[k],
                recv_sem=v_recv.at[block * 4 + vir],
                device_id=target,
                device_id_type=MESH,
            ).start()

    def t_copy(k, src, slab, peer):
        return pltpu.make_async_remote_copy(
            src_ref=src,
            dst_ref=tg_ref.at[slab],
            send_sem=t_send.at[k],
            recv_sem=t_recv.at[k],
            device_id=peer,
            device_id_type=MESH,
        )

    far = (vir + 2) % 4
    t_across = t_copy(0, tg_ref.at[vir], vir, across)
    t_near = t_copy(1, tg_ref.at[vir], vir, sibling)
    t_pass = t_copy(2, tg_ref.at[far], far, sibling)
    t_in.wait()
    both = jnp.concatenate(split(t_buf[...]), axis=1)
    tg_ref[vir] = compacted(pick_ref[...], both, ((1,), (1,)), ij_ref[...], most)

    def v_copy(part, dz, dx, child):
        zl, xs = (u + NZ - dz) % NZ, (x + NX - dx) % NX
        here = vg_ref.at[zl * NX + xs, pl.ds(*PARTS[part])]
        leaf = LEAVES[part][child]
        return pltpu.make_async_remote_copy(
            src_ref=here,
            dst_ref=here,
            send_sem=v_send.at[dz * len(PARTS) + part],
            recv_sem=leaf_recv.at[zl * len(PARTS) + part] if leaf else v_recv.at[(zl * NX + xs) * 4 + part],
            device_id=away(child // 4 - dz, child % 4 - dx),
            device_id_type=MESH,
        )

    def wait_all(part, count, sem):
        if count:
            here = vg_ref.at[pl.ds(0, count), pl.ds(*PARTS[part])]
            pltpu.make_async_copy(here, here, sem).wait()

    t_across.start()
    t_near.start()
    for n, (part, dz, dx, below, arrivals) in enumerate(EVENTS):
        zl, xs = (u + NZ - dz) % NZ, (x + NX - dx) % NX
        if n == int(len(EVENTS) * 0.35):
            t_across.wait_recv()
            t_pass.start()

        @pl.when(zl < 4)
        def _():
            for k in arrivals:
                rows = (k * ROWS, ROWS) if dz == 0 and dx == 0 else PARTS[part]
                here = vg_ref.at[zl * NX + xs, pl.ds(*rows)]
                pltpu.make_async_copy(here, here, v_recv.at[(zl * NX + xs) * 4 + k]).wait()
            for child in below:
                v_copy(part, dz, dx, child).start()

    t_near.wait_recv()
    t_pass.wait_recv()
    most = jnp.float32(0)
    for s in range(SLABS):
        most = jnp.maximum(most, jnp.max(tg_ref[s, CAP:ROWS, :]))
    rounds_ref[0, 0] = (most.astype(jnp.int32) + (CAP - 1)) // CAP
    row = lax.broadcasted_iota(jnp.int32, tg_ref.shape[1:], 0)
    parts = [jnp.where(row == CAP, 0.0, tg_ref[s]) for s in range(SLABS)]
    high, low = split(jnp.concatenate(parts, axis=0).T)
    left_ref[...] = jnp.concatenate([high, high, low], axis=1)
    labels = ij_ref[...].astype(F32)
    mask_ref[...] = jnp.broadcast_to(labels, (128, labels.shape[1])).T

    for copy in (t_across, t_near, t_pass):
        copy.wait_send()
    for k in range(2):
        here = mine & (y_lo == k)

        @pl.when(jnp.logical_not(here))
        def _():
            pltpu.make_async_remote_copy(
                src_ref=vc_ref,
                dst_ref=vg_ref.at[block, pl.ds(vir * ROWS, ROWS)],
                send_sem=y_send.at[k],
                recv_sem=v_recv.at[block * 4 + vir],
                device_id=(at(k, z, x), 2 * y_lo + z // 4),
                device_id_type=MESH,
            ).wait_send()

    for dz in range(NZ):

        @pl.when((u + NZ - dz) % NZ < 4)
        def _():
            for part in range(len(PARTS)):
                wait_all(part, SENT[part][dz], v_send.at[dz * len(PARTS) + part])

    for dz in (0, 1, 7, 2, 6, 3, 5, 4):
        zl = (u + NZ - dz) % NZ

        @pl.when(zl < 4)
        def _():
            for part in range(len(PARTS)):
                wait_all(part, sum(LEAVES[part][4 * dz : 4 * dz + 4]), leaf_recv.at[zl * len(PARTS) + part])


def spread(round_index, t, v, ij, cd, ab):
    n_ij, n_cd = t.shape
    anywhere = pl.BlockSpec(memory_space=pl.ANY)
    vmem = pl.BlockSpec(memory_space=pltpu.VMEM)
    smem = pl.BlockSpec(memory_space=pltpu.SMEM)
    return pl.pallas_call(
        spread_kernel,
        out_shape=(
            jax.ShapeDtypeStruct((16, SLABS * ROWS, v.shape[1]), F32),
            jax.ShapeDtypeStruct((n_ij, 3 * SLABS * ROWS), BF16),
            jax.ShapeDtypeStruct((n_ij, 128), F32),
            jax.ShapeDtypeStruct((1, 1), jnp.int32),
        ),
        in_specs=[smem, anywhere, anywhere, vmem, vmem, vmem],
        out_specs=(anywhere, vmem, vmem, smem),
        scratch_shapes=[
            pltpu.VMEM(t.shape, F32),
            pltpu.VMEM(v.shape, F32),
            pltpu.VMEM((ROWS, v.shape[1]), F32),
            pltpu.VMEM((SLABS, ROWS, n_ij), F32),
            pltpu.VMEM((G * ROWS, 2 * n_cd), BF16),
            pltpu.SemaphoreType.DMA((NZ * len(PARTS),)),
            pltpu.SemaphoreType.DMA((16 * len(PARTS),)),
            pltpu.SemaphoreType.DMA((4 * len(PARTS),)),
            pltpu.SemaphoreType.DMA((2,)),
            pltpu.SemaphoreType.DMA((3,)),
            pltpu.SemaphoreType.DMA((3,)),
            pltpu.SemaphoreType.DMA((2,)),
        ],
        compiler_params=pltpu.CompilerParams(
            collective_id=0, has_side_effects=True, vmem_limit_bytes=24 << 20
        ),
        name="spread",
    )(round_index, t, v, ij[None, :], cd[None, :], ab[None, :])


def product_kernel(left_ref, vg_ref, mask_ref, out_hbm, out_buf, out_sem):
    copies = []
    for step in range(4):
        blocks = range(step * 4, step * 4 + 4)
        value = jnp.concatenate([vg_ref[b] for b in blocks], axis=1)
        labels = jnp.concatenate([vg_ref[b, CAP:ROWS, :] for b in blocks], axis=1)
        high, low = split(value)
        right = jnp.concatenate([high, low, high], axis=0)
        total = jnp.dot(left_ref[...], right, preferred_element_type=F32)
        same = jnp.concatenate([mask_ref[...]] * 4, axis=1) == labels
        out_buf[step] = jnp.where(same, total, 0.0)
        columns = pl.ds(step * 512, 512)
        copy = pltpu.make_async_copy(out_buf.at[step], out_hbm.at[:, columns], out_sem.at[step])
        copy.start()
        copies.append(copy)
    for copy in copies:
        copy.wait()


def product(left, vg, mask):
    n_ij = left.shape[0]
    vmem = pl.BlockSpec(memory_space=pltpu.VMEM)
    return pl.pallas_call(
        product_kernel,
        out_shape=jax.ShapeDtypeStruct((n_ij, 2048), F32),
        in_specs=[vmem, vmem, vmem],
        out_specs=pl.BlockSpec(memory_space=pl.ANY),
        scratch_shapes=[pltpu.VMEM((4, n_ij, 512), F32), pltpu.SemaphoreType.DMA((4,))],
        compiler_params=pltpu.CompilerParams(vmem_limit_bytes=24 << 20),
        name="product",
    )(left, vg, mask)


def per_device(*args):
    def one_round(index):
        vg, left, mask, rounds = spread(index.reshape(1, 1), *args)
        return product(left, vg, mask), rounds

    ladder, rounds = one_round(jnp.int32(0))

    def more(state):
        return state[0] < rounds[0, 0]

    def next_round(state):
        index, total = state
        return index + 1, total + one_round(index)[0]

    return lax.while_loop(more, next_round, (jnp.int32(1), ladder))[1]


def solution(mesh):
    in_specs = (P("occ", "vir"), P("vir", "occ"), P("occ"), P("vir"), P("occ"))
    out_specs = P("occ", "vir")
    return jax.shard_map(
        per_device, mesh=mesh, in_specs=in_specs, out_specs=out_specs, check_vma=False
    )
```

time: 44.2 us -> 40.4 us (0.914)
  Pallas kernels: 43.3 us -> 39.2 us
    pallas_call x1, Pallas kernels: 37.5 us -> 35.3 us  [spread(): pl.pallas_call(spread_kernel, out_shape=(jax.ShapeDtypeStruct((16, SLABS...]
    pallas_call x1, Pallas kernels: 5.78 us -> 3.9 us  [product(): pl.pallas_call(product_kernel, out_shape=jax.ShapeDtypeStruct((n_ij, 2048...]
where the time goes in v4:
time: 40.4 us; the launch traced here: 40.3 us
  Pallas kernels  39.2 us (97%)
  loops' own time  0.81 us (2%)
    pallas_call x1, Pallas kernels, spread(): pl.pallas_call(spread_kernel, out_shape=(jax.ShapeDtypeStruct((16, SLABS...  35.3 us
    pallas_call x1, Pallas kernels, product(): pl.pallas_call(product_kernel, out_shape=jax.ShapeDtypeStruct((n_ij, 2048...  3.9 us
    another operation x1, loops' own time, per_device(): return lax.while_loop(more, next_round, (jnp.int32(1), ladder))[1]  0.81 us

profile of v4, /device:TPU:1, one launch (start us, length us, event | category | flops | bytes accessed | tf_op | source)
XLA Modules:
  0.0 40.3 jit_solution(3300686236557585032)
XLA Ops:
  0.0 35.3 %spread.2 = (f32[16,384,128]{2,1,0:T(8,128)S(1)}, bf16[512,1152]{1,0:T(8,128)(2,1)S(1)}, f32[512,128]{1,0:T(8,128)S(1)}, s32[1,1]{1,0:T(1,128)}) custom-call(s32[1,1]{1,0:T(1,128)} %constant.2.clone.1.round_ref, f32[512,512]{1,0:T(8,128)} %t_hbm.1, f32[512,128]{1,0:T(8,128)} %v_hbm.1, s32[1,512]{1,0:T(1,128)} %bitcast.17, s32[1,512]{1,0:T(1,128)} %bitcast.19, ...), custom_call_target="tpu_custom_call" | custom-call | tf_op jit(solution)/shard_map/spread/pallas_call | solution.py:289
  35.3 0.0 copy-start.2
  35.3 0.0 copy-start.3
  35.3 0.0 copy-start.4
  35.4 0.0 copy-start.5
  35.4 0.0 copy-start.6
  35.4 3.9 %product.2 = f32[512,2048]{1,0:T(8,128)} custom-call(bf16[512,1152]{1,0:T(8,128)(2,1)S(1)} %get-tuple-element.55.left_ref, f32[16,384,128]{2,1,0:T(8,128)S(1)} %get-tuple-element.56.vg_ref, f32[512,128]{1,0:T(8,128)S(1)} %get-tuple-element.57.mask_ref), custom_call_target="tpu_custom_call" | custom-call | tf_op jit(solution)/shard_map/product/pallas_call | solution.py:342
  39.3 0.0 copy-done.2
  39.3 0.0 copy-done.3
  39.3 0.0 copy-done.4
  39.3 0.0 copy-done.5
  39.3 0.0 copy-done.6
  39.3 0.8 %while.10 = (s32[]{:T(128)}, f32[512,2048]{1,0:T(8,128)}, s32[1,1]{1,0:T(1,128)}, s32[512]{0:T(512)S(1)}, s32[512]{0:T(512)S(1)}, /*index=5*/s32[128]{0:T(128)S(...) while((s32[]{:T(128)}, f32[512,2048]{1,0:T(8,128)}, s32[1,1]{1,0:T(1,128)}, s32[512]{0:T(512)S(1)}, ...), condition=%wide.region_1.0_spmd, body=%wide.region_0.0_spmd.sunk | while | flops 1048578 | bytes 46137500 | solution.py:367
Async XLA Ops:
  35.3 4.0 %copy-start.2 = (f32[512,512]{1,0:T(8,128)S(1)}, f32[512,512]{1,0:T(8,128)}, u32[]{:S(2)}) copy-start(f32[512,512]{1,0:T(8,128)} %t_hbm.1) | copy-start | bytes 3145732
  35.3 4.0 %copy-start.3 = (f32[512,128]{1,0:T(8,128)S(1)}, f32[512,128]{1,0:T(8,128)}, u32[]{:S(2)}) copy-start(f32[512,128]{1,0:T(8,128)} %v_hbm.1) | copy-start | bytes 786436
  35.3 4.0 %copy-start.4 = (s32[512]{0:T(512)S(1)}, s32[512]{0:T(512)}, u32[]{:S(2)}) copy-start(s32[512]{0:T(512)} %param.9) | copy-start | bytes 6148
  35.4 4.0 %copy-start.5 = (s32[512]{0:T(512)S(1)}, s32[512]{0:T(512)}, u32[]{:S(2)}) copy-start(s32[512]{0:T(512)} %param.10) | copy-start | bytes 6148
  35.4 4.0 %copy-start.6 = (s32[128]{0:T(128)S(1)}, s32[128]{0:T(128)}, u32[]{:S(2)}) copy-start(s32[128]{0:T(128)} %param.11) | copy-start | bytes 1540

commit v5 on v4

--- a/solution.py
+++ b/solution.py
@@ -94,6 +94,7 @@
 
 
 EVENTS, LEAVES = spread_plan()
+LATE = (0, 0, 4 * (NZ - 1))
 
 
 SENT = [
@@ -113,14 +114,36 @@
     return functools.reduce(jnp.logical_or, [u == v for v in sorted(values)])
 
 
+ROW_ORDER = [
+    sorted(range(4), key=lambda zl: (min((u - zl) % NZ, (zl - u) % NZ), zl)) for u in range(NZ)
+]
+
+
+def row_order(u):
+    digits = [sum(zl * 4**j for j, zl in enumerate(rows)) for rows in ROW_ORDER]
+    return functools.reduce(jnp.add, [jnp.where(u == k, d, 0) for k, d in enumerate(digits)])
+
+
+def row_product(left_ref, vg_ref, mask_ref, zl):
+    blocks = [zl * NX + b for b in range(NX)]
+    value = jnp.concatenate([vg_ref[b] for b in blocks], axis=1)
+    labels = jnp.concatenate([vg_ref[b, CAP:ROWS, :] for b in blocks], axis=1)
+    high, low = split(value)
+    right = jnp.concatenate([high, low, high], axis=0)
+    total = jnp.dot(left_ref[...], right, preferred_element_type=F32)
+    return jnp.where(jnp.concatenate([mask_ref[...]] * NX, axis=1) == labels, total, 0.0)
+
+
 def spread_kernel(
-    round_ref, t_hbm, v_hbm, ij_ref, cd_ref, ab_ref, vg_ref, left_ref, mask_ref, rounds_ref,
-    t_buf, v_buf, vc_ref, tg_ref, pick_ref, v_send, v_recv, leaf_recv, y_send, t_send, t_recv, in_sem,
+    round_hbm, t_hbm, v_hbm, ij_hbm, cd_hbm, ab_hbm, vg_ref, left_ref, mask_ref, rounds_hbm,
+    round_ref, t_buf, v_buf, ij_ref, cd_ref, ab_ref, rounds_ref, vc_ref, tg_ref, pick_ref, v_send, v_recv, leaf_recv, y_send, t_send, t_recv, in_sem, late_sem,
 ):
-    t_in = pltpu.make_async_copy(t_hbm, t_buf, in_sem.at[0])
-    v_in = pltpu.make_async_copy(v_hbm, v_buf, in_sem.at[1])
-    v_in.start()
-    t_in.start()
+    inputs = (cd_hbm, cd_ref), (round_hbm, round_ref), (v_hbm, v_buf), (ab_hbm, ab_ref)
+    inputs += (t_hbm, t_buf), (ij_hbm, ij_ref)
+    copies_in = [pltpu.make_async_copy(*pair, in_sem.at[k]) for k, pair in enumerate(inputs)]
+    cd_in, round_in, v_in, ab_in, t_in, ij_in = copies_in
+    for copy in copies_in:
+        copy.start()
     occ, vir = lax.axis_index("occ"), lax.axis_index("vir")
     y_lo, z, x = occ // (NX * NZ), (occ // NX) % NZ, occ % NX
     y_hi, core = vir // 2, vir % 2
@@ -144,22 +167,33 @@
     for peer in (sibling, across):
         ready_for(peer)
     heard = 4 - mine.astype(jnp.int32)
+    first_row, last_row = (u == 0) & (core == 0), (u == 7) & (core == 0)
+    pl.when(first_row)(lambda: ready_for(away(-1, 0)))
+    heard += last_row.astype(jnp.int32) - first_row.astype(jnp.int32)
     for (dz, dx), senders in STEPS.items():
-        source = (u + NZ - dz) % NZ
-        pl.when(among(source, senders))(lambda: ready_for(away(-dz, -dx)))
+        takes = among((u + NZ - dz) % NZ, senders)
+        if (dz, dx) == (NZ - 1, 0):
+            takes = takes & jnp.logical_not(last_row)
+        pl.when(takes)(lambda: ready_for(away(-dz, -dx)))
         heard += among(u, senders).astype(jnp.int32)
     for k in range(4):
         pl.when(owner & jnp.logical_not(mine & (vir == k)))(
             lambda: ready_for((at(y_hi, z, x), k))
         )
 
-    pick2, most = picker(round_ref[0, 0], cd_ref[...])
+    cd_in.wait()
+    round_in.wait()
+    pick2, most = picker(round_ref[:, 0:1], cd_ref[...])
     pick_ref[...] = pick2
+    ab_in.wait()
     ab = ab_ref[...]
     v_in.wait()
     both = jnp.concatenate(split(v_buf[...]), axis=0)
     vc_ref[...] = compacted(pick2, both, ((1,), (0,)), ab, ab.astype(F32))
     pl.semaphore_wait(barrier, heard)
+    pl.when(last_row)(
+        lambda: pl.semaphore_signal(late_sem, 1, device_id=away(1, 0), device_id_type=MESH)
+    )
 
     block = (z % 4) * NX + x
     for k in range(2):
@@ -198,6 +232,7 @@
     t_near = t_copy(1, tg_ref.at[vir], vir, sibling)
     t_pass = t_copy(2, tg_ref.at[far], far, sibling)
     t_in.wait()
+    ij_in.wait()
     both = jnp.concatenate(split(t_buf[...]), axis=1)
     tg_ref[vir] = compacted(pick_ref[...], both, ((1,), (1,)), ij_ref[...], most)
 
@@ -234,7 +269,20 @@
                 here = vg_ref.at[zl * NX + xs, pl.ds(*rows)]
                 pltpu.make_async_copy(here, here, v_recv.at[(zl * NX + xs) * 4 + k]).wait()
             for child in below:
-                v_copy(part, dz, dx, child).start()
+                copy = v_copy(part, dz, dx, child)
+                if (dz, dx, child) == LATE:
+                    pl.when(jnp.logical_not(first_row))(copy.start)
+                else:
+                    copy.start()
+
+        if n == 3:
+
+            @pl.when(first_row)
+            def _():
+                pl.semaphore_wait(late_sem, 1)
+                for event in EVENTS[:4]:
+                    if LATE[2] in event[3]:
+                        v_copy(event[0], *LATE).start()
 
     t_near.wait_recv()
     t_pass.wait_recv()
@@ -242,6 +290,8 @@
     for s in range(SLABS):
         most = jnp.maximum(most, jnp.max(tg_ref[s, CAP:ROWS, :]))
     rounds_ref[0, 0] = (most.astype(jnp.int32) + (CAP - 1)) // CAP
+    rounds_out = pltpu.make_async_copy(rounds_ref, rounds_hbm, in_sem.at[len(inputs)])
+    rounds_out.start()
     row = lax.broadcasted_iota(jnp.int32, tg_ref.shape[1:], 0)
     parts = [jnp.where(row == CAP, 0.0, tg_ref[s]) for s in range(SLABS)]
     high, low = split(jnp.concatenate(parts, axis=0).T)
@@ -249,6 +299,7 @@
     labels = ij_ref[...].astype(F32)
     mask_ref[...] = jnp.broadcast_to(labels, (128, labels.shape[1])).T
 
+    rounds_out.wait()
     for copy in (t_across, t_near, t_pass):
         copy.wait_send()
     for k in range(2):
@@ -272,20 +323,23 @@
             for part in range(len(PARTS)):
                 wait_all(part, SENT[part][dz], v_send.at[dz * len(PARTS) + part])
 
-    for dz in (0, 1, 7, 2, 6, 3, 5, 4):
-        zl = (u + NZ - dz) % NZ
-
-        @pl.when(zl < 4)
-        def _():
-            for part in range(len(PARTS)):
-                wait_all(part, sum(LEAVES[part][4 * dz : 4 * dz + 4]), leaf_recv.at[zl * len(PARTS) + part])
+    def row_complete(zl):
+        for dz in range(NZ):
+
+            @pl.when((zl + dz) % NZ == u)
+            def _():
+                for part in range(len(PARTS)):
+                    leaves = sum(LEAVES[part][4 * dz : 4 * dz + 4])
+                    wait_all(part, leaves, leaf_recv.at[zl * len(PARTS) + part])
+
+    for j in range(4):
+        row_complete((row_order(u) // 4**j) % 4)
 
 
 def spread(round_index, t, v, ij, cd, ab):
     n_ij, n_cd = t.shape
     anywhere = pl.BlockSpec(memory_space=pl.ANY)
     vmem = pl.BlockSpec(memory_space=pltpu.VMEM)
-    smem = pl.BlockSpec(memory_space=pltpu.SMEM)
     return pl.pallas_call(
         spread_kernel,
         out_shape=(
@@ -294,11 +348,16 @@
             jax.ShapeDtypeStruct((n_ij, 128), F32),
             jax.ShapeDtypeStruct((1, 1), jnp.int32),
         ),
-        in_specs=[smem, anywhere, anywhere, vmem, vmem, vmem],
-        out_specs=(anywhere, vmem, vmem, smem),
+        in_specs=[anywhere] * 6,
+        out_specs=(vmem, vmem, vmem, anywhere),
         scratch_shapes=[
+            pltpu.VMEM(round_index.shape, jnp.int32),
             pltpu.VMEM(t.shape, F32),
             pltpu.VMEM(v.shape, F32),
+            pltpu.VMEM((1, n_ij), jnp.int32),
+            pltpu.VMEM((1, n_cd), jnp.int32),
+            pltpu.VMEM((1, v.shape[1]), jnp.int32),
+            pltpu.SMEM((1, 1), jnp.int32),
             pltpu.VMEM((ROWS, v.shape[1]), F32),
             pltpu.VMEM((SLABS, ROWS, n_ij), F32),
             pltpu.VMEM((G * ROWS, 2 * n_cd), BF16),
@@ -308,10 +367,11 @@
             pltpu.SemaphoreType.DMA((2,)),
             pltpu.SemaphoreType.DMA((3,)),
             pltpu.SemaphoreType.DMA((3,)),
-            pltpu.SemaphoreType.DMA((2,)),
+            pltpu.SemaphoreType.DMA((7,)),
+            pltpu.SemaphoreType.REGULAR,
         ],
         compiler_params=pltpu.CompilerParams(
-            collective_id=0, has_side_effects=True, vmem_limit_bytes=24 << 20
+            collective_id=0, has_side_effects=True, vmem_limit_bytes=32 << 20
         ),
         name="spread",
     )(round_index, t, v, ij[None, :], cd[None, :], ab[None, :])
@@ -319,17 +379,11 @@
 
 def product_kernel(left_ref, vg_ref, mask_ref, out_hbm, out_buf, out_sem):
     copies = []
-    for step in range(4):
-        blocks = range(step * 4, step * 4 + 4)
-        value = jnp.concatenate([vg_ref[b] for b in blocks], axis=1)
-        labels = jnp.concatenate([vg_ref[b, CAP:ROWS, :] for b in blocks], axis=1)
-        high, low = split(value)
-        right = jnp.concatenate([high, low, high], axis=0)
-        total = jnp.dot(left_ref[...], right, preferred_element_type=F32)
-        same = jnp.concatenate([mask_ref[...]] * 4, axis=1) == labels
-        out_buf[step] = jnp.where(same, total, 0.0)
-        columns = pl.ds(step * 512, 512)
-        copy = pltpu.make_async_copy(out_buf.at[step], out_hbm.at[:, columns], out_sem.at[step])
+    width = out_buf.shape[2]
+    for zl in range(4):
+        out_buf[zl] = row_product(left_ref, vg_ref, mask_ref, zl)
+        columns = pl.ds(zl * width, width)
+        copy = pltpu.make_async_copy(out_buf.at[zl], out_hbm.at[:, columns], out_sem.at[zl])
         copy.start()
         copies.append(copy)
     for copy in copies:
@@ -337,14 +391,14 @@
 
 
 def product(left, vg, mask):
-    n_ij = left.shape[0]
+    n_ij, width = left.shape[0], NX * vg.shape[2]
     vmem = pl.BlockSpec(memory_space=pltpu.VMEM)
     return pl.pallas_call(
         product_kernel,
-        out_shape=jax.ShapeDtypeStruct((n_ij, 2048), F32),
-        in_specs=[vmem, vmem, vmem],
+        out_shape=jax.ShapeDtypeStruct((n_ij, 4 * width), F32),
+        in_specs=[vmem] * 3,
         out_specs=pl.BlockSpec(memory_space=pl.ANY),
-        scratch_shapes=[pltpu.VMEM((4, n_ij, 512), F32), pltpu.SemaphoreType.DMA((4,))],
+        scratch_shapes=[pltpu.VMEM((4, n_ij, width), F32), pltpu.SemaphoreType.DMA((4,))],
         compiler_params=pltpu.CompilerParams(vmem_limit_bytes=24 << 20),
         name="product",
     )(left, vg, mask)
@@ -352,7 +406,7 @@
 
 def per_device(*args):
     def one_round(index):
-        vg, left, mask, rounds = spread(index.reshape(1, 1), *args)
+        vg, left, mask, rounds = spread(jnp.full((1, 128), index), *args)
         return product(left, vg, mask), rounds
 
     ladder, rounds = one_round(jnp.int32(0))

time: 40.4 us -> 38.9 us (0.963)
  Pallas kernels: 39.2 us -> 37.7 us
    pallas_call x1, Pallas kernels: 35.3 us -> 33.8 us  [spread(): pl.pallas_call(spread_kernel, out_shape=(jax.ShapeDtypeStruct((16, SLABS...]
where the time goes in v5:
time: 38.9 us; the launch traced here: 38.8 us
  Pallas kernels  37.7 us (97%)
  loops' own time  0.81 us (2%)
    pallas_call x1, Pallas kernels, spread(): pl.pallas_call(spread_kernel, out_shape=(jax.ShapeDtypeStruct((16, SLABS...  33.8 us
    pallas_call x1, Pallas kernels, product(): pl.pallas_call(product_kernel, out_shape=jax.ShapeDtypeStruct((n_ij, 4 *...  3.9 us
    another operation x1, loops' own time, per_device(): return lax.while_loop(more, next_round, (jnp.int32(1), ladder))[1]  0.81 us

profile of v5, /device:TPU:1, one launch (start us, length us, event | category | flops | bytes accessed | tf_op | source)
XLA Modules:
  0.0 38.8 jit_solution(679200252484756577)
XLA Ops:
  0.0 33.8 %spread.2 = (f32[16,384,128]{2,1,0:T(8,128)S(1)}, bf16[512,1152]{1,0:T(8,128)(2,1)S(1)}, f32[512,128]{1,0:T(8,128)S(1)}, s32[1,1]{1,0:T(1,128)}) custom-call(s32[1,128]{1,0:T(1,128)S(1)} %broadcast_in_dim.24.round_hbm, f32[512,512]{1,0:T(8,128)} %t_hbm.1, f32[512,128]{1,0:T(8,128)} %v_hbm.1, s32[1,512]{1,0:T(1,128)} %bitcast.14, s32[1,512]{1,0:T(1,128)} %bitcast.16, ...), custom_call_target="tpu_custom_call" | custom-call | tf_op jit(solution)/shard_map/spread/pallas_call | solution.py:343
  33.8 0.0 copy-start.2
  33.8 0.0 copy-start.3
  33.9 0.0 copy-start.4
  33.9 0.0 copy-start.5
  33.9 0.0 copy-start.6
  33.9 3.9 %product.2 = f32[512,2048]{1,0:T(8,128)} custom-call(bf16[512,1152]{1,0:T(8,128)(2,1)S(1)} %get-tuple-element.55.left_ref, f32[16,384,128]{2,1,0:T(8,128)S(1)} %get-tuple-element.56.vg_ref, f32[512,128]{1,0:T(8,128)S(1)} %get-tuple-element.57.mask_ref), custom_call_target="tpu_custom_call" | custom-call | tf_op jit(solution)/shard_map/product/pallas_call | solution.py:396
  37.8 0.0 copy-done.2
  37.8 0.0 copy-done.3
  37.8 0.0 copy-done.4
  37.8 0.0 copy-done.5
  37.8 0.0 copy-done.6
  37.8 0.8 %while.10 = (s32[]{:T(128)}, f32[512,2048]{1,0:T(8,128)}, s32[1,1]{1,0:T(1,128)}, s32[512]{0:T(512)S(1)}, s32[512]{0:T(512)S(1)}, /*index=5*/s32[128]{0:T(128)S(...) while((s32[]{:T(128)}, f32[512,2048]{1,0:T(8,128)}, s32[1,1]{1,0:T(1,128)}, s32[512]{0:T(512)S(1)}, ...), condition=%wide.region_1.0_spmd, body=%wide.region_0.0_spmd.sunk | while | flops 1048578 | bytes 46138016 | solution.py:421
  (1 shorter events, 0.0 us)
Async XLA Ops:
  33.8 4.0 %copy-start.2 = (f32[512,512]{1,0:T(8,128)S(1)}, f32[512,512]{1,0:T(8,128)}, u32[]{:S(2)}) copy-start(f32[512,512]{1,0:T(8,128)} %t_hbm.1) | copy-start | bytes 3145732
  33.8 4.0 %copy-start.3 = (f32[512,128]{1,0:T(8,128)S(1)}, f32[512,128]{1,0:T(8,128)}, u32[]{:S(2)}) copy-start(f32[512,128]{1,0:T(8,128)} %v_hbm.1) | copy-start | bytes 786436
  33.9 4.0 %copy-start.4 = (s32[512]{0:T(512)S(1)}, s32[512]{0:T(512)}, u32[]{:S(2)}) copy-start(s32[512]{0:T(512)} %param.9) | copy-start | bytes 6148
  33.9 4.0 %copy-start.5 = (s32[512]{0:T(512)S(1)}, s32[512]{0:T(512)}, u32[]{:S(2)}) copy-start(s32[512]{0:T(512)} %param.10) | copy-start | bytes 6148
  33.9 4.0 %copy-start.6 = (s32[128]{0:T(128)S(1)}, s32[128]{0:T(128)}, u32[]{:S(2)}) copy-start(s32[128]{0:T(128)} %param.11) | copy-start | bytes 1540

commit v6 on v5

--- a/solution.py
+++ b/solution.py
@@ -114,16 +114,6 @@
     return functools.reduce(jnp.logical_or, [u == v for v in sorted(values)])
 
 
-ROW_ORDER = [
-    sorted(range(4), key=lambda zl: (min((u - zl) % NZ, (zl - u) % NZ), zl)) for u in range(NZ)
-]
-
-
-def row_order(u):
-    digits = [sum(zl * 4**j for j, zl in enumerate(rows)) for rows in ROW_ORDER]
-    return functools.reduce(jnp.add, [jnp.where(u == k, d, 0) for k, d in enumerate(digits)])
-
-
 def row_product(left_ref, vg_ref, mask_ref, zl):
     blocks = [zl * NX + b for b in range(NX)]
     value = jnp.concatenate([vg_ref[b] for b in blocks], axis=1)
@@ -196,7 +186,7 @@
     )
 
     block = (z % 4) * NX + x
-    for k in range(2):
+    for k in (1, 0):
         target = (at(k, z, x), 2 * y_lo + z // 4)
         here = mine & (y_lo == k)
 
@@ -236,16 +226,20 @@
     both = jnp.concatenate(split(t_buf[...]), axis=1)
     tg_ref[vir] = compacted(pick_ref[...], both, ((1,), (1,)), ij_ref[...], most)
 
+    near = {step: away(*step) for step in STEPS}
+    row_at = [(u + NZ - dz) % NZ for dz in range(NZ)]
+    column_at = [(x + NX - dx) % NX for dx in range(NX)]
+
     def v_copy(part, dz, dx, child):
-        zl, xs = (u + NZ - dz) % NZ, (x + NX - dx) % NX
+        zl, xs = row_at[dz], column_at[dx]
         here = vg_ref.at[zl * NX + xs, pl.ds(*PARTS[part])]
         leaf = LEAVES[part][child]
         return pltpu.make_async_remote_copy(
             src_ref=here,
             dst_ref=here,
             send_sem=v_send.at[dz * len(PARTS) + part],
-            recv_sem=leaf_recv.at[zl * len(PARTS) + part] if leaf else v_recv.at[(zl * NX + xs) * 4 + part],
-            device_id=away(child // 4 - dz, child % 4 - dx),
+            recv_sem=leaf_recv.at[zl] if leaf else v_recv.at[(zl * NX + xs) * 4 + part],
+            device_id=near[(child // 4 - dz) % NZ, (child % 4 - dx) % NX],
             device_id_type=MESH,
         )
 
@@ -254,11 +248,12 @@
             here = vg_ref.at[pl.ds(0, count), pl.ds(*PARTS[part])]
             pltpu.make_async_copy(here, here, sem).wait()
 
-    t_across.start()
-    t_near.start()
     for n, (part, dz, dx, below, arrivals) in enumerate(EVENTS):
-        zl, xs = (u + NZ - dz) % NZ, (x + NX - dx) % NX
+        zl, xs = row_at[dz], column_at[dx]
         if n == int(len(EVENTS) * 0.35):
+            t_across.start()
+            t_near.start()
+        if n == int(len(EVENTS) * 0.75):
             t_across.wait_recv()
             t_pass.start()
 
@@ -318,22 +313,20 @@
 
     for dz in range(NZ):
 
-        @pl.when((u + NZ - dz) % NZ < 4)
+        @pl.when(row_at[dz] < 4)
         def _():
             for part in range(len(PARTS)):
                 wait_all(part, SENT[part][dz], v_send.at[dz * len(PARTS) + part])
 
-    def row_complete(zl):
-        for dz in range(NZ):
-
-            @pl.when((zl + dz) % NZ == u)
-            def _():
-                for part in range(len(PARTS)):
-                    leaves = sum(LEAVES[part][4 * dz : 4 * dz + 4])
-                    wait_all(part, leaves, leaf_recv.at[zl * len(PARTS) + part])
-
-    for j in range(4):
-        row_complete((row_order(u) // 4**j) % 4)
+    for dz in (0, 1, 7, 2, 6, 3, 5, 4):
+        leaf_rows = sum(
+            PARTS[part][1] * sum(LEAVES[part][4 * dz : 4 * dz + 4]) for part in range(len(PARTS))
+        )
+
+        @pl.when(row_at[dz] < 4)
+        def _():
+            here = vg_ref.at[pl.ds(0, 4), pl.ds(0, leaf_rows // 4)]
+            pltpu.make_async_copy(here, here, leaf_recv.at[row_at[dz]]).wait()
 
 
 def spread(round_index, t, v, ij, cd, ab):
@@ -363,7 +356,7 @@
             pltpu.VMEM((G * ROWS, 2 * n_cd), BF16),
             pltpu.SemaphoreType.DMA((NZ * len(PARTS),)),
             pltpu.SemaphoreType.DMA((16 * len(PARTS),)),
-            pltpu.SemaphoreType.DMA((4 * len(PARTS),)),
+            pltpu.SemaphoreType.DMA((4,)),
             pltpu.SemaphoreType.DMA((2,)),
             pltpu.SemaphoreType.DMA((3,)),
             pltpu.SemaphoreType.DMA((3,)),

time: 38.9 us -> 38.3 us (0.985)
  Pallas kernels: 37.7 us -> 37.1 us
    pallas_call x1, Pallas kernels: 33.8 us -> 33.2 us  [spread(): pl.pallas_call(spread_kernel, out_shape=(jax.ShapeDtypeStruct((16, SLABS...]
where the time goes in v6:
time: 38.3 us; the launch traced here: 38.2 us
  Pallas kernels  37.1 us (97%)
  loops' own time  0.81 us (2%)
    pallas_call x1, Pallas kernels, spread(): pl.pallas_call(spread_kernel, out_shape=(jax.ShapeDtypeStruct((16, SLABS...  33.2 us
    pallas_call x1, Pallas kernels, product(): pl.pallas_call(product_kernel, out_shape=jax.ShapeDtypeStruct((n_ij, 4 *...  3.9 us
    another operation x1, loops' own time, per_device(): return lax.while_loop(more, next_round, (jnp.int32(1), ladder))[1]  0.81 us

profile of v6, /device:TPU:1, one launch (start us, length us, event | category | flops | bytes accessed | tf_op | source)
XLA Modules:
  0.0 38.2 jit_solution(13644078999221311196)
XLA Ops:
  0.0 33.2 %spread.2 = (f32[16,384,128]{2,1,0:T(8,128)S(1)}, bf16[512,1152]{1,0:T(8,128)(2,1)S(1)}, f32[512,128]{1,0:T(8,128)S(1)}, s32[1,1]{1,0:T(1,128)}) custom-call(s32[1,128]{1,0:T(1,128)S(1)} %broadcast_in_dim.24.round_hbm, f32[512,512]{1,0:T(8,128)} %t_hbm.1, f32[512,128]{1,0:T(8,128)} %v_hbm.1, s32[1,512]{1,0:T(1,128)} %bitcast.14, s32[1,512]{1,0:T(1,128)} %bitcast.16, ...), custom_call_target="tpu_custom_call" | custom-call | tf_op jit(solution)/shard_map/spread/pallas_call | solution.py:336
  33.2 0.0 copy-start.2
  33.2 0.0 copy-start.3
  33.2 0.0 copy-start.4
  33.3 0.0 copy-start.5
  33.3 0.0 copy-start.6
  33.3 3.9 %product.2 = f32[512,2048]{1,0:T(8,128)} custom-call(bf16[512,1152]{1,0:T(8,128)(2,1)S(1)} %get-tuple-element.55.left_ref, f32[16,384,128]{2,1,0:T(8,128)S(1)} %get-tuple-element.56.vg_ref, f32[512,128]{1,0:T(8,128)S(1)} %get-tuple-element.57.mask_ref), custom_call_target="tpu_custom_call" | custom-call | tf_op jit(solution)/shard_map/product/pallas_call | solution.py:389
  37.2 0.0 copy-done.2
  37.2 0.0 copy-done.3
  37.2 0.0 copy-done.4
  37.2 0.0 copy-done.5
  37.2 0.0 copy-done.6
  37.2 0.8 %while.10 = (s32[]{:T(128)}, f32[512,2048]{1,0:T(8,128)}, s32[1,1]{1,0:T(1,128)}, s32[512]{0:T(512)S(1)}, s32[512]{0:T(512)S(1)}, /*index=5*/s32[128]{0:T(128)S(...) while((s32[]{:T(128)}, f32[512,2048]{1,0:T(8,128)}, s32[1,1]{1,0:T(1,128)}, s32[512]{0:T(512)S(1)}, ...), condition=%wide.region_1.0_spmd, body=%wide.region_0.0_spmd.sunk | while | flops 1048578 | bytes 46138016 | solution.py:414
  (1 shorter events, 0.0 us)
Async XLA Ops:
  33.2 4.0 %copy-start.2 = (f32[512,512]{1,0:T(8,128)S(1)}, f32[512,512]{1,0:T(8,128)}, u32[]{:S(2)}) copy-start(f32[512,512]{1,0:T(8,128)} %t_hbm.1) | copy-start | bytes 3145732
  33.2 4.0 %copy-start.3 = (f32[512,128]{1,0:T(8,128)S(1)}, f32[512,128]{1,0:T(8,128)}, u32[]{:S(2)}) copy-start(f32[512,128]{1,0:T(8,128)} %v_hbm.1) | copy-start | bytes 786436
  33.2 4.0 %copy-start.4 = (s32[512]{0:T(512)S(1)}, s32[512]{0:T(512)}, u32[]{:S(2)}) copy-start(s32[512]{0:T(512)} %param.9) | copy-start | bytes 6148
  33.3 4.0 %copy-start.5 = (s32[512]{0:T(512)S(1)}, s32[512]{0:T(512)}, u32[]{:S(2)}) copy-start(s32[512]{0:T(512)} %param.10) | copy-start | bytes 6148
  33.3 4.0 %copy-start.6 = (s32[128]{0:T(128)S(1)}, s32[128]{0:T(128)}, u32[]{:S(2)}) copy-start(s32[128]{0:T(128)} %param.11) | copy-start | bytes 1540

commit v7 on v6

--- a/solution.py
+++ b/solution.py
@@ -221,11 +221,6 @@
     t_across = t_copy(0, tg_ref.at[vir], vir, across)
     t_near = t_copy(1, tg_ref.at[vir], vir, sibling)
     t_pass = t_copy(2, tg_ref.at[far], far, sibling)
-    t_in.wait()
-    ij_in.wait()
-    both = jnp.concatenate(split(t_buf[...]), axis=1)
-    tg_ref[vir] = compacted(pick_ref[...], both, ((1,), (1,)), ij_ref[...], most)
-
     near = {step: away(*step) for step in STEPS}
     row_at = [(u + NZ - dz) % NZ for dz in range(NZ)]
     column_at = [(x + NX - dx) % NX for dx in range(NX)]
@@ -250,6 +245,11 @@
 
     for n, (part, dz, dx, below, arrivals) in enumerate(EVENTS):
         zl, xs = row_at[dz], column_at[dx]
+        if n == 4:
+            t_in.wait()
+            ij_in.wait()
+            both = jnp.concatenate(split(t_buf[...]), axis=1)
+            tg_ref[vir] = compacted(pick_ref[...], both, ((1,), (1,)), ij_ref[...], most)
         if n == int(len(EVENTS) * 0.35):
             t_across.start()
             t_near.start()

time: 38.3 us -> 38.3 us (level)
  no operation moved by 1% of the time
where the time goes in v7:
time: 38.3 us; the launch traced here: 38.2 us
  Pallas kernels  37.1 us (97%)
  loops' own time  0.81 us (2%)
    pallas_call x1, Pallas kernels, spread(): pl.pallas_call(spread_kernel, out_shape=(jax.ShapeDtypeStruct((16, SLABS...  33.2 us
    pallas_call x1, Pallas kernels, product(): pl.pallas_call(product_kernel, out_shape=jax.ShapeDtypeStruct((n_ij, 4 *...  3.9 us
    another operation x1, loops' own time, per_device(): return lax.while_loop(more, next_round, (jnp.int32(1), ladder))[1]  0.81 us

profile of v7, /device:TPU:1, one launch (start us, length us, event | category | flops | bytes accessed | tf_op | source)
XLA Modules:
  0.0 38.2 jit_solution(6283869232869940538)
XLA Ops:
  0.0 33.2 %spread.2 = (f32[16,384,128]{2,1,0:T(8,128)S(1)}, bf16[512,1152]{1,0:T(8,128)(2,1)S(1)}, f32[512,128]{1,0:T(8,128)S(1)}, s32[1,1]{1,0:T(1,128)}) custom-call(s32[1,128]{1,0:T(1,128)S(1)} %broadcast_in_dim.24.round_hbm, f32[512,512]{1,0:T(8,128)} %t_hbm.1, f32[512,128]{1,0:T(8,128)} %v_hbm.1, s32[1,512]{1,0:T(1,128)} %bitcast.14, s32[1,512]{1,0:T(1,128)} %bitcast.16, ...), custom_call_target="tpu_custom_call" | custom-call | tf_op jit(solution)/shard_map/spread/pallas_call | solution.py:336
  33.2 0.0 copy-start.2
  33.2 0.0 copy-start.3
  33.2 0.0 copy-start.4
  33.3 0.0 copy-start.5
  33.3 0.0 copy-start.6
  33.3 3.9 %product.2 = f32[512,2048]{1,0:T(8,128)} custom-call(bf16[512,1152]{1,0:T(8,128)(2,1)S(1)} %get-tuple-element.55.left_ref, f32[16,384,128]{2,1,0:T(8,128)S(1)} %get-tuple-element.56.vg_ref, f32[512,128]{1,0:T(8,128)S(1)} %get-tuple-element.57.mask_ref), custom_call_target="tpu_custom_call" | custom-call | tf_op jit(solution)/shard_map/product/pallas_call | solution.py:389
  37.2 0.0 copy-done.2
  37.2 0.0 copy-done.3
  37.2 0.0 copy-done.4
  37.2 0.0 copy-done.5
  37.2 0.0 copy-done.6
  37.2 0.8 %while.10 = (s32[]{:T(128)}, f32[512,2048]{1,0:T(8,128)}, s32[1,1]{1,0:T(1,128)}, s32[512]{0:T(512)S(1)}, s32[512]{0:T(512)S(1)}, /*index=5*/s32[128]{0:T(128)S(...) while((s32[]{:T(128)}, f32[512,2048]{1,0:T(8,128)}, s32[1,1]{1,0:T(1,128)}, s32[512]{0:T(512)S(1)}, ...), condition=%wide.region_1.0_spmd, body=%wide.region_0.0_spmd.sunk | while | flops 1048578 | bytes 46138016 | solution.py:414
  (1 shorter events, 0.0 us)
Async XLA Ops:
  33.2 4.0 %copy-start.2 = (f32[512,512]{1,0:T(8,128)S(1)}, f32[512,512]{1,0:T(8,128)}, u32[]{:S(2)}) copy-start(f32[512,512]{1,0:T(8,128)} %t_hbm.1) | copy-start | bytes 3145732
  33.2 4.0 %copy-start.3 = (f32[512,128]{1,0:T(8,128)S(1)}, f32[512,128]{1,0:T(8,128)}, u32[]{:S(2)}) copy-start(f32[512,128]{1,0:T(8,128)} %v_hbm.1) | copy-start | bytes 786436
  33.2 4.0 %copy-start.4 = (s32[512]{0:T(512)S(1)}, s32[512]{0:T(512)}, u32[]{:S(2)}) copy-start(s32[512]{0:T(512)} %param.9) | copy-start | bytes 6148
  33.3 4.0 %copy-start.5 = (s32[512]{0:T(512)S(1)}, s32[512]{0:T(512)}, u32[]{:S(2)}) copy-start(s32[512]{0:T(512)} %param.10) | copy-start | bytes 6148
  33.3 4.0 %copy-start.6 = (s32[128]{0:T(128)S(1)}, s32[128]{0:T(128)}, u32[]{:S(2)}) copy-start(s32[128]{0:T(128)} %param.11) | copy-start | bytes 1540
